TPU v7x, 512 devices: a whole 4x8x8 slice. The times are simulated.
512 devices in a mesh: gx: 32 (over x, y), gy: 16 (over z, core).
Axes of the slice: x: 4, y: 8, z: 8, core: 2. Of those that a mesh axis runs over, the one named last changes fastest.
Arguments:
- u_star: float32 [2, 1, 1536, 4096], P(None, None, 'gy', 'gx'), may hold values from -6 to 6
- v_star: float32 [2, 1, 1536, 4096], P(None, None, 'gy', 'gx'), may hold values from -6 to 6
- w_star: float32 [2, 1, 1536, 4096], P(None, None, 'gy', 'gx'), may hold values from -6 to 6
- cell_width: float32 [1536], P('gy'), may hold values from 0.0003841146 to 0.0055403646
- face_weight: float32 [1536], P('gy'), may hold values from 179.712 to 2560.512
Outputs:
- u_new: float32 [2, 1, 1536, 4096], P(None, None, 'gy', 'gx')
- v_new: float32 [2, 1, 1536, 4096], P(None, None, 'gy', 'gx')
- w_new: float32 [2, 1, 1536, 4096], P(None, None, 'gy', 'gx')
All inputs are finite; a program needn't handle non-finite values.
Results may differ from a plain program's by a relative error of at most 0.0012.
Values sent between devices are 32-bit elements; how exact they have to be, the bound alone decides.
No kernel may reach another device: no remote copies, remote signals or barrier semaphores. Data moves between devices by JAX's collectives and lax.ppermute only.
A program may use at most 64 MiB of HBM per device.

v0:
```python
import math

import jax
import jax.numpy as jnp
from jax import lax
from jax.sharding import PartitionSpec as P

FLOW_FACTOR = 0.5
SPAN_FACTOR = 1.0
TWO_PI = 2.0 * math.pi
HIGHEST = lax.Precision.HIGHEST


def swapped(value, axis, bit):
    mask = 2**bit
    pairs = [(source, source ^ mask) for source in range(lax.axis_size(axis))]
    return lax.ppermute(value, axis, pairs)


def from_behind(array, axis, by):
    length = lax.axis_size(axis)
    pairs = [(i, i + by) for i in range(length) if 0 <= i + by < length]
    return lax.ppermute(array, axis, pairs)


def complex_scale(values, cosine, sine_part):
    return jnp.stack(
        [values[0] * cosine - values[1] * sine_part, values[0] * sine_part + values[1] * cosine]
    )


def dft_matrix(length, direction):
    index_vals = jnp.arange(length)
    product = index_vals[:, None] * index_vals[None, :] % length
    angles = direction * TWO_PI * product.astype(jnp.float32) / length
    cosine = jnp.cos(angles)
    sine_part = jnp.sin(angles)
    return jnp.stack([jnp.stack([cosine, sine_part]), jnp.stack([-sine_part, cosine])])


def along_last(values, dft_mat):
    return jnp.einsum("c...m,cemk->e...k", values, dft_mat, precision=HIGHEST)


def twiddle(values, first_idx, direction, full_len):
    cols_idx = jnp.arange(values.shape[-1])
    product = first_idx * cols_idx % full_len
    angles = direction * TWO_PI * product.astype(jnp.float32) / full_len
    return complex_scale(values, jnp.cos(angles), jnp.sin(angles))


def reversed_bits(index_val, levels):
    result = jnp.zeros((), jnp.int32)
    for bit_idx in range(levels):
        result = result + index_val // (1 << bit_idx) % 2 * (1 << levels - 1 - bit_idx)
    return result


def forward_transform(fields):
    node_count = lax.axis_size("gx")
    my_rank = lax.axis_index("gx")
    x_cols = fields.shape[-1]
    full_len = node_count * x_cols
    forward_mat = dft_matrix(x_cols, -1.0)
    levels = node_count.bit_length() - 1
    current = fields
    for section_idx in range(levels):
        bit_pos = levels - 1 - section_idx
        half_span = 1 << bit_pos
        partner = swapped(current, "gx", bit_pos)
        angles = -TWO_PI * (my_rank % half_span).astype(jnp.float32) / (2 * half_span)
        rotated = complex_scale(partner - current, jnp.cos(angles), jnp.sin(angles))
        current = jnp.where(my_rank // half_span % 2 == 0, current + partner, rotated)
    first_idx = reversed_bits(my_rank, levels)
    spectrum = along_last(twiddle(current, first_idx, -1.0, full_len), forward_mat)
    return (spectrum, first_idx)


def inverse_transform(spectrum, first_idx):
    node_count = lax.axis_size("gx")
    my_rank = lax.axis_index("gx")
    x_cols = spectrum.shape[-1]
    full_len = node_count * x_cols
    begun = twiddle(along_last(spectrum, dft_matrix(x_cols, 1.0)), first_idx, 1.0, full_len)
    levels = node_count.bit_length() - 1
    current = begun
    for section_idx in range(levels):
        half_span = 1 << section_idx
        partner = swapped(current, "gx", section_idx)
        angles = TWO_PI * (my_rank % half_span).astype(jnp.float32) / (2 * half_span)
        cosine = jnp.cos(angles)
        sine_part = jnp.sin(angles)
        lower_val = current + complex_scale(partner, cosine, sine_part)
        upper_val = partner - complex_scale(current, cosine, sine_part)
        current = jnp.where(my_rank // half_span % 2 == 0, lower_val, upper_val)
    return current / full_len


def tridiagonal(diagonal, below_g, above_g, right_side):

    def downward(state_in, row_items):
        prev_c, prev_d = state_in
        diag_row, below_row, above_row, right_row = row_items
        pivot_val = diag_row + below_row * prev_c
        new_c = -above_row / pivot_val
        new_d = (right_row + below_row * prev_d) / pivot_val
        return ((new_c, new_d), (new_c, new_d))

    zero_state = (jnp.zeros_like(diagonal[0]), jnp.zeros_like(right_side[0]))
    ignored, (upper_c, upper_d) = lax.scan(
        downward, zero_state, (diagonal, below_g, above_g, right_side)
    )

    def upward(state_in, row_items):
        row_c, row_d = row_items
        solved_val = row_d - row_c * state_in
        return (solved_val, solved_val)

    ignored_last, solved = lax.scan(
        upward, jnp.zeros_like(right_side[0]), (upper_c, upper_d), reverse=True
    )
    return solved


def link_forward(coupling, ratio_cur, offset_cur):
    lo_first, lo_last, hi_first, hi_last, base_first, base_last = coupling
    pivot_val = 1.0 - lo_first * ratio_cur
    ratio_out = hi_last + lo_last * ratio_cur * hi_first / pivot_val
    offset_out = (
        base_last
        + lo_last * offset_cur
        + lo_last * ratio_cur * (base_first + lo_first * offset_cur) / pivot_val
    )
    return (ratio_out, offset_out)


def link_back(coupling, ratio_cur, offset_cur, value_next):
    lo_first, lo_last, hi_first, hi_last, base_first, base_last = coupling
    pivot_val = 1.0 - lo_first * ratio_cur
    return (base_first + lo_first * offset_cur + hi_first * value_next) / pivot_val


def per_device(u_star, v_star, w_star, cell_width, face_weight):
    kcount = u_star.shape[1]
    rows_here = u_star.shape[2]
    x_cols = u_star.shape[3]
    nodes_x = lax.axis_size("gx")
    nodes_y = lax.axis_size("gy")
    row_rank = lax.axis_index("gy")
    full_len = nodes_x * x_cols
    span_wave = ((jnp.arange(kcount) + 1) * SPAN_FACTOR).astype(jnp.float32)
    span_col = span_wave[:, None, None]
    below_v, below_g = from_behind((v_star[:, :, -1:, :], face_weight[-1:]), "gy", 1)
    g_low = below_g[0]
    v_prev = jnp.concatenate([below_v, v_star[:, :, :-1, :]], axis=2)
    widths = cell_width[None, :, None]
    div_real = (v_star[0] - v_prev[0]) / widths - span_col * w_star[1]
    div_imag = (v_star[1] - v_prev[1]) / widths + span_col * w_star[0]
    fields = jnp.stack([u_star, jnp.stack([div_real, div_imag])], axis=1)
    spectrum, first_idx = forward_transform(fields)
    wave_idx = first_idx + nodes_x * jnp.arange(x_cols)
    signed = jnp.where(wave_idx < full_len // 2, wave_idx, wave_idx - full_len)
    flow_wave = signed.astype(jnp.float32) * FLOW_FACTOR
    u_hat = spectrum[:, 0]
    div_hat = spectrum[:, 1]
    rhs_real = div_hat[0] - flow_wave * u_hat[1]
    rhs_imag = div_hat[1] + flow_wave * u_hat[0]
    right_side = -widths * jnp.stack([rhs_real, rhs_imag])
    right_rows = jnp.moveaxis(right_side, 2, 0)
    row_idx = jnp.arange(rows_here)
    unit_first = jnp.broadcast_to(
        (row_idx == 0).astype(jnp.float32)[:, None, None, None], (rows_here, 1, kcount, x_cols)
    )
    unit_last = jnp.broadcast_to(
        (row_idx == rows_here - 1).astype(jnp.float32)[:, None, None, None],
        (rows_here, 1, kcount, x_cols),
    )
    stacked_rhs = jnp.concatenate([right_rows, unit_first, unit_last], axis=1)
    g_high = jnp.where(row_rank == nodes_y - 1, jnp.zeros_like(face_weight[-1]), face_weight[-1])
    inner_g = face_weight[:-1]
    zero_one = jnp.zeros((1,), jnp.float32)
    upper_full = jnp.concatenate([inner_g, g_high[None]])
    lower_full = jnp.concatenate([g_low[None], inner_g])
    inner_below = jnp.concatenate([zero_one, inner_g])
    inner_above = jnp.concatenate([inner_g, zero_one])
    wave_sq = flow_wave[None, :] ** 2 + span_wave[:, None] ** 2
    diagonal = (upper_full + lower_full)[:, None, None] + wave_sq[None] * cell_width[:, None, None]
    solved = tridiagonal(diagonal, inner_below, inner_above, stacked_rhs)
    base_part = solved[:, :2]
    left_spike = solved[:, 2]
    right_spike = solved[:, 3]
    coupling = (
        g_low * left_spike[0],
        g_low * left_spike[-1],
        g_high * right_spike[0],
        g_high * right_spike[-1],
        base_part[0],
        base_part[-1],
    )
    zero_ratio = jnp.zeros((kcount, x_cols), jnp.float32)
    zero_offset = jnp.zeros((2, kcount, x_cols), jnp.float32)
    first_out = link_forward(coupling, zero_ratio, zero_offset)

    def eliminate_step(counter, state_in):
        sent_pair = from_behind((state_in[2], state_in[3]), "gy", 1)
        renewed = link_forward(coupling, sent_pair[0], sent_pair[1])
        return (sent_pair[0], sent_pair[1], renewed[0], renewed[1])

    chain_state = lax.fori_loop(
        0, nodes_y - 1, eliminate_step, (zero_ratio, zero_offset, first_out[0], first_out[1])
    )
    ratio_in = chain_state[0]
    offset_in = chain_state[1]
    first_value = link_back(coupling, ratio_in, offset_in, zero_offset)

    def substitute_step(counter, state_in):
        arrived = from_behind(state_in[1], "gy", -1)
        return (arrived, link_back(coupling, ratio_in, offset_in, arrived))

    outcome = lax.fori_loop(0, nodes_y - 1, substitute_step, (zero_offset, first_value))
    value_next = outcome[0]
    value_here = outcome[1]
    edge_prev = ratio_in * value_here + offset_in
    potential = (
        base_part
        + g_low * edge_prev[None] * left_spike[:, None]
        + g_high * value_next[None] * right_spike[:, None]
    )
    flow_grad = jnp.stack([-flow_wave * potential[:, 1], flow_wave * potential[:, 0]], axis=1)
    pot_next = jnp.concatenate([potential[1:], value_next[None]], axis=0)
    grad_rows = upper_full[:, None, None, None] * (pot_next - potential)
    span_grad = jnp.stack(
        [-span_wave[:, None] * potential[:, 1], span_wave[:, None] * potential[:, 0]], axis=1
    )
    gradients = jnp.stack([flow_grad, grad_rows, span_grad])
    spectral = jnp.transpose(gradients, (2, 0, 3, 1, 4))
    physical = inverse_transform(spectral, first_idx)
    return (u_star - physical[:, 0], v_star - physical[:, 1], w_star - physical[:, 2])


def solution(mesh):
    return jax.shard_map(
        per_device,
        mesh=mesh,
        in_specs=(
            P(None, None, "gy", "gx"),
            P(None, None, "gy", "gx"),
            P(None, None, "gy", "gx"),
            P("gy"),
            P("gy"),
        ),
        out_specs=(P(None, None, "gy", "gx"), P(None, None, "gy", "gx"), P(None, None, "gy", "gx")),
        check_vma=False,
    )
```

profile of v0, /device:TPU:196, one launch (start us, length us, event | category | flops | bytes accessed | tf_op | source)
XLA Modules:
  0.0 700.6 jit_solution(1052271947430197157)
XLA Ops:
  3.9 5.6 collective-permute-start.3
  13.7 2.4 collective-permute-start.5
  16.4 7.5 %collective-permute-done.5 = f32[2,2,1,96,128]{4,3,0,1,2:T(8,128)S(1)} collective-permute-done((f32[2,2,1,96,128]{4,3,0,1,2:T(8,128)S(1)}, f32[2,2,1,96,128]{4,3,0,1,2:T(8,128)S(1)}, u32[]{:S(2)}, u32[]{:S(2)}) %collective-permute-start.5) | collective-permute-done | bytes 196640 | tf_op jit(solution)/shard_map/ppermute | solution.py:17
  24.0 3.1 collective-permute-start.6
  27.1 4.7 collective-permute-done.6
  32.0 7.7 %collective-permute-start.7 = (f32[2,2,1,96,128]{4,3,0,1,2:T(8,128)S(1)}, f32[2,2,1,96,128]{4,3,0,1,2:T(8,128)S(1)}, u32[]{:S(2)}, u32[]{:S(2)}) collective-permute-start(f32[2,2,1,96,128]{4,3,0,1,2:T(8,128)S(1)} %maximum_select_fusion.1), channel_id=1, source_target_pairs={{0,64},{16,80},{32,96},{48,112},{64,0},{80,16},{96,32},{112,48},{1... | collective-permute-start | bytes 589832 | tf_op jit(solution)/shard_map/ppermute | solution.py:17
  39.8 6.9 collective-permute-done.7
  46.8 4.9 collective-permute-start.8
  52.4 6.0 collective-permute-done.8
  58.5 2.4 collective-permute-start.9
  61.2 5.2 collective-permute-done.9
  67.3 322.9 %while.70 = (s32[]{:T(128)}, f32[1,128]{1,0:T(1,128)S(1)}, f32[4,1,128]{2,1,0:T(1,128)S(1)}, f32[96,1,128]{2,1,0:T(1,128)S(1)}, f32[96,4,1,128]{3,1,2,0:T(4,128)...) while((s32[]{:T(128)}, f32[1,128]{1,0:T(1,128)S(1)}, ...), condition=%wide.region_1.2_spmd.clone.clone, body=%wide.region_0.1_spmd.clone.sunk.clone | while | flops 2564 | bytes 13472 | solution.py:110
  390.2 8.4 %while.71 = (s32[]{:T(128)}, f32[4,1,128]{2,1,0:T(1,128)S(1)}, f32[96,4,1,128]{3,1,2,0:T(4,128)S(1)}, f32[96,4,1,128]{3,1,2,0:T(4,128)S(1)}, f32[96,1,128]{2,1,0:T(1,128)S(1)}) while((s32[]{:T(128)}, f32[4,1,128]{2,1,0:T(1,128)S(1)}, f32[96,4,1,128]{3,1,2,0:T(4,128)S(1)}, f32[96,4,1,128]{3,1,2,0:T(4,128)S(1)}, ...), condition=%wide.region_3.4_spmd.clone.clone, body=%wide.region_2.3_spmd.clone.sunk.clone | while | flops 1540 | bytes 15967 | solution.py:119
  400.9 127.0 %while.68 = (s32[]{:T(128)}, f32[1,128]{1,0:T(1,128)}, f32[2,1,128]{2,1,0:T(1,128)}, f32[1,128]{1,0:T(1,128)S(1)}, f32[2,1,128]{2,1,0:T(1,128)S(1)}, /*index=5*/...) while((s32[]{:T(128)}, f32[1,128]{1,0:T(1,128)}, ...), condition=%wide.region_5.6_spmd.clone, body=%wide.region_4.5_spmd.sunk.clone | while | flops 2562 | bytes 22773 | solution.py:209
  402.8 3.5 collective-permute-start.1
  410.2 4.7 collective-permute-start.1
  416.3 2.2 collective-permute-start
  418.5 5.0 collective-permute-start.1
  424.8 2.2 collective-permute-start
  427.1 5.0 collective-permute-start.1
  433.4 2.2 collective-permute-start
  435.7 5.0 collective-permute-start.1
  442.0 2.2 collective-permute-start
  444.3 5.0 collective-permute-start.1
  450.6 2.2 collective-permute-start
  452.8 5.0 collective-permute-start.1
  459.2 2.2 collective-permute-start
  461.4 5.0 collective-permute-start.1
  467.8 2.2 collective-permute-start
  470.0 5.0 collective-permute-start.1
  476.4 2.2 collective-permute-start
  478.6 5.0 collective-permute-start.1
  485.0 2.2 collective-permute-start
  487.2 5.0 collective-permute-start.1
  495.8 5.0 collective-permute-start.1
  504.4 5.0 collective-permute-start.1
  513.0 5.0 collective-permute-start.1
  521.6 5.0 collective-permute-start.1
  529.9 96.8 %while.69 = (s32[]{:T(128)}, f32[2,1,128]{2,1,0:T(1,128)}, f32[2,1,128]{2,1,0:T(1,128)S(1)}, f32[1,128]{1,0:T(1,128)S(1)}, f32[2,1,128]{2,1,0:T(1,128)S(1)}, /*i...) while((s32[]{:T(128)}, f32[2,1,128]{2,1,0:T(1,128)}, ...), condition=%wide.region_7.8_spmd.clone, body=%wide.region_6.7_spmd.sunk.clone | while | flops 1410 | bytes 15001 | solution.py:220
  533.7 3.6 collective-permute-start.2
  537.3 2.3 collective-permute-done.2
  540.1 2.6 collective-permute-start.2
  542.7 3.5 collective-permute-done.2
  548.7 4.2 collective-permute-done.2
  555.3 4.2 collective-permute-done.2
  562.0 4.2 collective-permute-done.2
  568.7 4.2 collective-permute-done.2
  575.3 4.2 collective-permute-done.2
  582.0 4.2 collective-permute-done.2
  588.7 4.2 collective-permute-done.2
  595.3 4.2 collective-permute-done.2
  602.0 4.2 collective-permute-done.2
  608.6 4.2 collective-permute-done.2
  615.3 4.2 collective-permute-done.2
  622.0 4.2 collective-permute-done.2
  630.9 6.9 collective-permute-done.10
  637.9 3.1 collective-permute-start.11
  641.2 15.5 %collective-permute-done.11 = f32[2,3,1,96,128]{4,3,1,0,2:T(8,128)S(1)} collective-permute-done((f32[2,3,1,96,128]{4,3,1,0,2:T(8,128)S(1)}, f32[2,3,1,96,128]{4,3,1,0,2:T(8,128)S(1)}, u32[]{:S(2)}, u32[]{:S(2)}) %collective-permute-start.11) | collective-permute-done | bytes 294944 | tf_op jit(solution)/shard_map/ppermute | solution.py:17
  656.9 5.5 collective-permute-start.12
  662.6 15.5 %collective-permute-done.12 = f32[2,3,1,96,128]{4,3,1,0,2:T(8,128)S(1)} collective-permute-done((f32[2,3,1,96,128]{4,3,1,0,2:T(8,128)S(1)}, f32[2,3,1,96,128]{4,3,1,0,2:T(8,128)S(1)}, u32[]{:S(2)}, u32[]{:S(2)}) %collective-permute-start.12) | collective-permute-done | bytes 294944 | tf_op jit(solution)/shard_map/ppermute | solution.py:17
  678.1 3.1 collective-permute-start.13
  681.5 7.1 %collective-permute-done.13 = f32[2,3,1,96,128]{4,3,1,0,2:T(8,128)S(1)} collective-permute-done((f32[2,3,1,96,128]{4,3,1,0,2:T(8,128)S(1)}, f32[2,3,1,96,128]{4,3,1,0,2:T(8,128)S(1)}, u32[]{:S(2)}, u32[]{:S(2)}) %collective-permute-start.13) | collective-permute-done | bytes 294944 | tf_op jit(solution)/shard_map/ppermute | solution.py:17
  688.7 2.4 collective-permute-start.14
  691.3 8.4 %collective-permute-done.14 = f32[2,3,1,96,128]{4,3,1,0,2:T(8,128)S(1)} collective-permute-done((f32[2,3,1,96,128]{4,3,1,0,2:T(8,128)S(1)}, f32[2,3,1,96,128]{4,3,1,0,2:T(8,128)S(1)}, u32[]{:S(2)}, u32[]{:S(2)}) %collective-permute-start.14) | collective-permute-done | bytes 294944 | tf_op jit(solution)/shard_map/ppermute | solution.py:17
  (1173 shorter events, 350.5 us)
Async XLA Ops:
  0.6 2.6 copy-start.10
  1.3 11.3 %collective-permute-start.4 = (f32[2,1,1,128]{3,2,0,1:T(1,128)S(1)}, f32[2,1,1,128]{3,2,0,1:T(1,128)S(1)}, u32[]{:S(2)}, u32[]{:S(2)}) collective-permute-start(f32[2,1,1,128]{3,2,0,1:T(1,128)S(1)} %slice.300), channel_id=1, source_target_pairs={{0,1},{1,2},{2,3},{3,4},{4,5},{5,6},{6,7},{7,8},{8,9},{9,10},{10,1... | collective-permute-start | bytes 3080 | tf_op jit(solution)/shard_map/ppermute | solution.py:23
  3.9 47.8 %collective-permute-start.3 = (f32[1]{0:T(128)}, f32[1]{0:T(128)}, u32[]{:S(2)}, u32[]{:S(2)}) collective-permute-start(f32[1]{0:T(128)} %slice.239), channel_id=1, source_target_pairs={{0,1},{1,2},{2,3},{3,4},{4,5},{5,6},{6,7},{7,8},{8,9},{9,10},{10,1... | collective-permute-start | bytes 20 | tf_op jit(solution)/shard_map/ppermute | solution.py:23
  10.3 2.4 copy-start.2
  10.5 2.1 copy-start.1
  11.3 0.7 copy-start.9
  12.8 0.9 copy-start
  13.7 10.2 %collective-permute-start.5 = (f32[2,2,1,96,128]{4,3,0,1,2:T(8,128)S(1)}, f32[2,2,1,96,128]{4,3,0,1,2:T(8,128)S(1)}, u32[]{:S(2)}, u32[]{:S(2)}) collective-permute-start(f32[2,2,1,96,128]{4,3,0,1,2:T(8,128)S(1)} %pad_maximum_fusion.1), channel_id=1, source_target_pairs={{0,256},{16,272},{32,288},{48,304},{64,320},{80,336},{96,352},{112... | collective-permute-start | bytes 589832 | tf_op jit(solution)/shard_map/ppermute | solution.py:17
  24.0 7.9 %collective-permute-start.6 = (f32[2,2,1,96,128]{4,3,0,1,2:T(8,128)S(1)}, f32[2,2,1,96,128]{4,3,0,1,2:T(8,128)S(1)}, u32[]{:S(2)}, u32[]{:S(2)}) collective-permute-start(f32[2,2,1,96,128]{4,3,0,1,2:T(8,128)S(1)} %maximum_select_fusion), channel_id=1, source_target_pairs={{0,128},{16,144},{32,160},{48,176},{64,192},{80,208},{96,224},{112... | collective-permute-start | bytes 589832 | tf_op jit(solution)/shard_map/ppermute | solution.py:17
  32.0 14.7 %collective-permute-start.7 = (f32[2,2,1,96,128]{4,3,0,1,2:T(8,128)S(1)}, f32[2,2,1,96,128]{4,3,0,1,2:T(8,128)S(1)}, u32[]{:S(2)}, u32[]{:S(2)}) collective-permute-start(f32[2,2,1,96,128]{4,3,0,1,2:T(8,128)S(1)} %maximum_select_fusion.1), channel_id=1, source_target_pairs={{0,64},{16,80},{32,96},{48,112},{64,0},{80,16},{96,32},{112,48},{1... | collective-permute-start | bytes 589832 | tf_op jit(solution)/shard_map/ppermute | solution.py:17
  46.8 11.6 %collective-permute-start.8 = (f32[2,2,1,96,128]{4,3,0,1,2:T(8,128)S(1)}, f32[2,2,1,96,128]{4,3,0,1,2:T(8,128)S(1)}, u32[]{:S(2)}, u32[]{:S(2)}) collective-permute-start(f32[2,2,1,96,128]{4,3,0,1,2:T(8,128)S(1)} %maximum_select_fusion.2), channel_id=1, source_target_pairs={{0,32},{16,48},{32,0},{48,16},{64,96},{80,112},{96,64},{112,80},{1... | collective-permute-start | bytes 589832 | tf_op jit(solution)/shard_map/ppermute | solution.py:17
  58.5 8.0 %collective-permute-start.9 = (f32[2,2,1,96,128]{4,3,0,1,2:T(8,128)S(1)}, f32[2,2,1,96,128]{4,3,0,1,2:T(8,128)S(1)}, u32[]{:S(2)}, u32[]{:S(2)}) collective-permute-start(f32[2,2,1,96,128]{4,3,0,1,2:T(8,128)S(1)} %maximum_select_fusion.3), channel_id=1, source_target_pairs={{0,16},{16,0},{32,48},{48,32},{64,80},{80,64},{96,112},{112,96},{1... | collective-permute-start | bytes 589832 | tf_op jit(solution)/shard_map/ppermute | solution.py:17
  400.9 5.4 collective-permute-start
  402.8 4.9 collective-permute-start.1
  408.3 6.6 collective-permute-start
  410.2 5.5 collective-permute-start.1
  416.3 7.2 %collective-permute-start = (f32[1,128]{1,0:T(1,128)S(1)}, f32[1,128]{1,0:T(1,128)S(1)}, u32[]{:S(2)}, u32[]{:S(2)}) collective-permute-start(f32[1,128]{1,0:T(1,128)S(1)} %get-tuple-element.879), channel_id=1, source_target_pairs={{0,1},{1,2},{2,3},{3,4},{4,5},{5,6},{6,7},{7,8},{8,9},{9,10},{10,1... | collective-permute-start | bytes 1544 | tf_op jit(solution)/shard_map/while/body/eval_jaxpr/ppermute | solution.py:23
  418.5 5.8 collective-permute-start.1
  424.8 7.2 %collective-permute-start = (f32[1,128]{1,0:T(1,128)S(1)}, f32[1,128]{1,0:T(1,128)S(1)}, u32[]{:S(2)}, u32[]{:S(2)}) collective-permute-start(f32[1,128]{1,0:T(1,128)S(1)} %get-tuple-element.879), channel_id=1, source_target_pairs={{0,1},{1,2},{2,3},{3,4},{4,5},{5,6},{6,7},{7,8},{8,9},{9,10},{10,1... | collective-permute-start | bytes 1544 | tf_op jit(solution)/shard_map/while/body/eval_jaxpr/ppermute | solution.py:23
  427.1 5.8 collective-permute-start.1
  433.4 7.2 %collective-permute-start = (f32[1,128]{1,0:T(1,128)S(1)}, f32[1,128]{1,0:T(1,128)S(1)}, u32[]{:S(2)}, u32[]{:S(2)}) collective-permute-start(f32[1,128]{1,0:T(1,128)S(1)} %get-tuple-element.879), channel_id=1, source_target_pairs={{0,1},{1,2},{2,3},{3,4},{4,5},{5,6},{6,7},{7,8},{8,9},{9,10},{10,1... | collective-permute-start | bytes 1544 | tf_op jit(solution)/shard_map/while/body/eval_jaxpr/ppermute | solution.py:23
  435.7 5.8 collective-permute-start.1
  442.0 7.2 %collective-permute-start = (f32[1,128]{1,0:T(1,128)S(1)}, f32[1,128]{1,0:T(1,128)S(1)}, u32[]{:S(2)}, u32[]{:S(2)}) collective-permute-start(f32[1,128]{1,0:T(1,128)S(1)} %get-tuple-element.879), channel_id=1, source_target_pairs={{0,1},{1,2},{2,3},{3,4},{4,5},{5,6},{6,7},{7,8},{8,9},{9,10},{10,1... | collective-permute-start | bytes 1544 | tf_op jit(solution)/shard_map/while/body/eval_jaxpr/ppermute | solution.py:23
  444.3 5.8 collective-permute-start.1
  450.6 7.2 %collective-permute-start = (f32[1,128]{1,0:T(1,128)S(1)}, f32[1,128]{1,0:T(1,128)S(1)}, u32[]{:S(2)}, u32[]{:S(2)}) collective-permute-start(f32[1,128]{1,0:T(1,128)S(1)} %get-tuple-element.879), channel_id=1, source_target_pairs={{0,1},{1,2},{2,3},{3,4},{4,5},{5,6},{6,7},{7,8},{8,9},{9,10},{10,1... | collective-permute-start | bytes 1544 | tf_op jit(solution)/shard_map/while/body/eval_jaxpr/ppermute | solution.py:23
  452.8 5.8 collective-permute-start.1
  459.2 7.2 %collective-permute-start = (f32[1,128]{1,0:T(1,128)S(1)}, f32[1,128]{1,0:T(1,128)S(1)}, u32[]{:S(2)}, u32[]{:S(2)}) collective-permute-start(f32[1,128]{1,0:T(1,128)S(1)} %get-tuple-element.879), channel_id=1, source_target_pairs={{0,1},{1,2},{2,3},{3,4},{4,5},{5,6},{6,7},{7,8},{8,9},{9,10},{10,1... | collective-permute-start | bytes 1544 | tf_op jit(solution)/shard_map/while/body/eval_jaxpr/ppermute | solution.py:23
  461.4 5.8 collective-permute-start.1
  467.8 7.2 %collective-permute-start = (f32[1,128]{1,0:T(1,128)S(1)}, f32[1,128]{1,0:T(1,128)S(1)}, u32[]{:S(2)}, u32[]{:S(2)}) collective-permute-start(f32[1,128]{1,0:T(1,128)S(1)} %get-tuple-element.879), channel_id=1, source_target_pairs={{0,1},{1,2},{2,3},{3,4},{4,5},{5,6},{6,7},{7,8},{8,9},{9,10},{10,1... | collective-permute-start | bytes 1544 | tf_op jit(solution)/shard_map/while/body/eval_jaxpr/ppermute | solution.py:23
  470.0 5.8 collective-permute-start.1
  476.4 7.2 %collective-permute-start = (f32[1,128]{1,0:T(1,128)S(1)}, f32[1,128]{1,0:T(1,128)S(1)}, u32[]{:S(2)}, u32[]{:S(2)}) collective-permute-start(f32[1,128]{1,0:T(1,128)S(1)} %get-tuple-element.879), channel_id=1, source_target_pairs={{0,1},{1,2},{2,3},{3,4},{4,5},{5,6},{6,7},{7,8},{8,9},{9,10},{10,1... | collective-permute-start | bytes 1544 | tf_op jit(solution)/shard_map/while/body/eval_jaxpr/ppermute | solution.py:23
  478.6 5.8 collective-permute-start.1
  485.0 7.2 %collective-permute-start = (f32[1,128]{1,0:T(1,128)S(1)}, f32[1,128]{1,0:T(1,128)S(1)}, u32[]{:S(2)}, u32[]{:S(2)}) collective-permute-start(f32[1,128]{1,0:T(1,128)S(1)} %get-tuple-element.879), channel_id=1, source_target_pairs={{0,1},{1,2},{2,3},{3,4},{4,5},{5,6},{6,7},{7,8},{8,9},{9,10},{10,1... | collective-permute-start | bytes 1544 | tf_op jit(solution)/shard_map/while/body/eval_jaxpr/ppermute | solution.py:23
  487.2 5.8 collective-permute-start.1
  493.6 7.2 %collective-permute-start = (f32[1,128]{1,0:T(1,128)S(1)}, f32[1,128]{1,0:T(1,128)S(1)}, u32[]{:S(2)}, u32[]{:S(2)}) collective-permute-start(f32[1,128]{1,0:T(1,128)S(1)} %get-tuple-element.879), channel_id=1, source_target_pairs={{0,1},{1,2},{2,3},{3,4},{4,5},{5,6},{6,7},{7,8},{8,9},{9,10},{10,1... | collective-permute-start | bytes 1544 | tf_op jit(solution)/shard_map/while/body/eval_jaxpr/ppermute | solution.py:23
  495.8 5.8 collective-permute-start.1
  502.2 7.2 %collective-permute-start = (f32[1,128]{1,0:T(1,128)S(1)}, f32[1,128]{1,0:T(1,128)S(1)}, u32[]{:S(2)}, u32[]{:S(2)}) collective-permute-start(f32[1,128]{1,0:T(1,128)S(1)} %get-tuple-element.879), channel_id=1, source_target_pairs={{0,1},{1,2},{2,3},{3,4},{4,5},{5,6},{6,7},{7,8},{8,9},{9,10},{10,1... | collective-permute-start | bytes 1544 | tf_op jit(solution)/shard_map/while/body/eval_jaxpr/ppermute | solution.py:23
  504.4 5.8 collective-permute-start.1
  510.7 7.2 %collective-permute-start = (f32[1,128]{1,0:T(1,128)S(1)}, f32[1,128]{1,0:T(1,128)S(1)}, u32[]{:S(2)}, u32[]{:S(2)}) collective-permute-start(f32[1,128]{1,0:T(1,128)S(1)} %get-tuple-element.879), channel_id=1, source_target_pairs={{0,1},{1,2},{2,3},{3,4},{4,5},{5,6},{6,7},{7,8},{8,9},{9,10},{10,1... | collective-permute-start | bytes 1544 | tf_op jit(solution)/shard_map/while/body/eval_jaxpr/ppermute | solution.py:23
  513.0 5.8 collective-permute-start.1
  519.3 7.2 %collective-permute-start = (f32[1,128]{1,0:T(1,128)S(1)}, f32[1,128]{1,0:T(1,128)S(1)}, u32[]{:S(2)}, u32[]{:S(2)}) collective-permute-start(f32[1,128]{1,0:T(1,128)S(1)} %get-tuple-element.879), channel_id=1, source_target_pairs={{0,1},{1,2},{2,3},{3,4},{4,5},{5,6},{6,7},{7,8},{8,9},{9,10},{10,1... | collective-permute-start | bytes 1544 | tf_op jit(solution)/shard_map/while/body/eval_jaxpr/ppermute | solution.py:23
  521.6 5.8 collective-permute-start.1
  528.6 0.7 copy-start.4
  529.9 3.2 collective-permute-start.2
  533.7 5.9 collective-permute-start.2
  540.1 6.1 collective-permute-start.2
  546.8 6.1 collective-permute-start.2
  553.4 6.1 collective-permute-start.2
  560.1 6.1 collective-permute-start.2
  566.7 6.1 collective-permute-start.2
  573.4 6.1 collective-permute-start.2
  580.1 6.1 collective-permute-start.2
  586.7 6.1 collective-permute-start.2
  593.4 6.1 collective-permute-start.2
  600.0 6.1 collective-permute-start.2
  606.7 6.1 collective-permute-start.2
  613.4 6.1 collective-permute-start.2
  620.0 6.1 collective-permute-start.2
  626.7 0.7 copy-start.6
  628.7 9.1 %collective-permute-start.10 = (f32[2,3,1,96,128]{4,3,1,0,2:T(8,128)S(1)}, f32[2,3,1,96,128]{4,3,1,0,2:T(8,128)S(1)}, u32[]{:S(2)}, u32[]{:S(2)}) collective-permute-start(f32[2,3,1,96,128]{4,3,1,0,2:T(8,128)S(1)} %pad_maximum_fusion), channel_id=1, source_target_pairs={{0,16},{16,0},{32,48},{48,32},{64,80},{80,64},{96,112},{112,96},{1... | collective-permute-start | bytes 884744 | tf_op jit(solution)/shard_map/ppermute | solution.py:17
  637.9 18.9 %collective-permute-start.11 = (f32[2,3,1,96,128]{4,3,1,0,2:T(8,128)S(1)}, f32[2,3,1,96,128]{4,3,1,0,2:T(8,128)S(1)}, u32[]{:S(2)}, u32[]{:S(2)}) collective-permute-start(f32[2,3,1,96,128]{4,3,1,0,2:T(8,128)S(1)} %fusion.14), channel_id=1, source_target_pairs={{0,32},{16,48},{32,0},{48,16},{64,96},{80,112},{96,64},{112,80},{1... | collective-permute-start | bytes 884744 | tf_op jit(solution)/shard_map/ppermute | solution.py:17
  656.9 21.1 %collective-permute-start.12 = (f32[2,3,1,96,128]{4,3,1,0,2:T(8,128)S(1)}, f32[2,3,1,96,128]{4,3,1,0,2:T(8,128)S(1)}, u32[]{:S(2)}, u32[]{:S(2)}) collective-permute-start(f32[2,3,1,96,128]{4,3,1,0,2:T(8,128)S(1)} %fusion.15), channel_id=1, source_target_pairs={{0,64},{16,80},{32,96},{48,112},{64,0},{80,16},{96,32},{112,48},{1... | collective-permute-start | bytes 884744 | tf_op jit(solution)/shard_map/ppermute | solution.py:17
  678.1 10.4 %collective-permute-start.13 = (f32[2,3,1,96,128]{4,3,1,0,2:T(8,128)S(1)}, f32[2,3,1,96,128]{4,3,1,0,2:T(8,128)S(1)}, u32[]{:S(2)}, u32[]{:S(2)}) collective-permute-start(f32[2,3,1,96,128]{4,3,1,0,2:T(8,128)S(1)} %fusion.16), channel_id=1, source_target_pairs={{0,128},{16,144},{32,160},{48,176},{64,192},{80,208},{96,224},{112... | collective-permute-start | bytes 884744 | tf_op jit(solution)/shard_map/ppermute | solution.py:17
  688.7 11.0 %collective-permute-start.14 = (f32[2,3,1,96,128]{4,3,1,0,2:T(8,128)S(1)}, f32[2,3,1,96,128]{4,3,1,0,2:T(8,128)S(1)}, u32[]{:S(2)}, u32[]{:S(2)}) collective-permute-start(f32[2,3,1,96,128]{4,3,1,0,2:T(8,128)S(1)} %fusion.17), channel_id=1, source_target_pairs={{0,256},{16,272},{32,288},{48,304},{64,320},{80,336},{96,352},{112... | collective-permute-start | bytes 884744 | tf_op jit(solution)/shard_map/ppermute | solution.py:17
  (46 other events, 24.7 us)
where the time goes:
time: 705 us; the launch traced here: 701 us
  starting transfers between devices  181 us (26%)
  local copies, waits for them, and re-layouts  159 us (23%)
  waiting for transfers between devices  146 us (21%)
  other arithmetic  143 us (20%)
  loops' own time  67.8 us (10%)
    ppermute x47, starting transfers between devices, from_behind(): return lax.ppermute(array, axis, pairs)  144 us
    dynamic_slice x288, local copies, waits for them, and re-layouts, tridiagonal(): lax.scan(downward, zero_state, (diagonal, below_g, above_g, right_side))  125 us
    ppermute x10, waiting for transfers between devices, swapped(): return lax.ppermute(value, axis, pairs)  83.7 us
    div x96, other arithmetic, downward(): new_d = (right_row + below_row * prev_d) / pivot_val  67.3 us
    dynamic_update_slice x96, other arithmetic, tridiagonal(): lax.scan(downward, zero_state, (diagonal, below_g, above_g, right_side))  66.8 us
    another operation x1, loops' own time, tridiagonal(): lax.scan(downward, zero_state, (diagonal, below_g, above_g, right_side))  62.9 us
    ppermute x47, waiting for transfers between devices, from_behind(): return lax.ppermute(array, axis, pairs)  61.9 us
    ppermute x10, starting transfers between devices, swapped(): return lax.ppermute(value, axis, pairs)  36.9 us
  transfers between devices with their start and end apart: 57, of which 40 were waited for; matrix products, arithmetic and copies ran while one was open for 1% of the time, Pallas kernels for 0%

commit v1 on v0

v1 whole, which is shorter than its diff:
```python
import functools
import math

import jax
import jax.numpy as jnp
import numpy as np
from jax import lax
from jax.experimental import pallas as pl
from jax.experimental.pallas import tpu as pltpu
from jax.sharding import PartitionSpec as P

FLOW_FACTOR = 0.5
SPAN_FACTOR = 1.0
KZ = SPAN_FACTOR
STANDIN = 16.0
HIGHEST = lax.Precision.HIGHEST
F32 = jnp.float32
VMEM = pl.BlockSpec(memory_space=pltpu.VMEM)
SEND_A, SEND_B, SEND_C, SEND_D = 16, 8, 8, 16


def tables(nodes, cols):
    full = nodes * cols

    def cos_sin(a, b, length):
        angle = 2.0 * np.pi * (np.outer(np.arange(a), np.arange(b)) % length) / length
        return np.cos(angle), np.sin(angle)

    c, s = cos_sin(nodes, nodes, nodes)
    across_f = np.block([[c, s], [-s, c]])
    across_i = np.block([[c, -s], [s, c]])
    c, s = cos_sin(cols, cols, cols)
    along_f = np.block([[c, -s], [s, c]])
    along_i = np.block([[c, s], [-s, c]]) / full
    turn = np.stack(cos_sin(nodes, cols, full))
    return [np.asarray(m, np.float32) for m in (across_f, across_i, along_f, along_i, turn)]


def dot(a, b):
    return lax.dot_general(a, b, (((1,), (0,)), ((), ())), precision=HIGHEST, preferred_element_type=F32)


def signed_half(wave, full):
    return jnp.where(wave < full // 2, wave, wave - full).astype(F32) * FLOW_FACTOR


def wavenumbers(nodes, cols):
    rank = lax.broadcasted_iota(jnp.int32, (nodes, cols), 0)
    place = lax.broadcasted_iota(jnp.int32, (nodes, cols), 1)
    return signed_half(rank + nodes * place, nodes * cols)


def column(row, rows, cols):
    here = lax.broadcasted_iota(jnp.int32, (rows, rows), 0)
    there = lax.broadcasted_iota(jnp.int32, (rows, rows), 1)
    one = jnp.sum(jnp.where(here == there, jnp.broadcast_to(row, (rows, rows)), 0.0), axis=1, keepdims=True)
    return jnp.broadcast_to(one, (rows, cols))


def prepare(nodes, u, v, w, width, weight, send, wide, heavy, tmp):
    rows, cols = u.shape[1:]
    per = rows // nodes
    h = column(width[...], rows, cols)
    wide[...] = h
    heavy[...] = column(weight[...], rows, cols)
    first = lax.broadcasted_iota(jnp.int32, (rows, cols), 0) == 0
    for part in range(2):
        tmp[part] = -h * u[part]
        now = v[part]
        below = jnp.where(first, 0.0, pltpu.roll(now, 1, 0))
        other = w[1 - part] * (h * KZ)
        tmp[2 + part] = below - now + (other if part == 0 else -other)
    for field in range(4):
        for t in range(per):
            send[pl.ds(field * per + t, nodes, stride=SEND_A), :] = tmp[field, pl.ds(t * nodes, nodes), :]
    for part in range(2):
        last = jnp.broadcast_to(v[part, rows - 1 : rows, :], (nodes, cols))
        send[pl.ds(4 * per + part, nodes, stride=SEND_A), :] = last
        send[pl.ds(4 * per + 2 + part, nodes, stride=SEND_A), :] = jnp.zeros_like(last)


def forward(nodes, per, got, across, along, turn, send, edge, pick):
    cols = got.shape[1]
    rank = lax.axis_index("gx")

    def slot(s):
        return got[pl.ds(s, nodes, stride=SEND_A), :]

    real = [slot(t) for t in range(per)] + [slot(2 * per + t) for t in range(per)] + [slot(4 * per)]
    imag = [slot(per + t) for t in range(per)] + [slot(3 * per + t) for t in range(per)] + [slot(4 * per + 1)]
    both = jnp.concatenate([jnp.concatenate(real, 1), jnp.concatenate(imag, 1)], 0)
    mixed = dot(across[...], both)
    c, s = turn[0], turn[1]
    turned = []
    for i in range(2 * per + 1):
        a = mixed[:nodes, i * cols : (i + 1) * cols]
        b = mixed[nodes:, i * cols : (i + 1) * cols]
        turned.append(jnp.concatenate([a * c + b * s, b * c - a * s], 1))
    pick[...] = turned[-1]
    mine = jnp.broadcast_to(pick[pl.ds(rank, 1), :], (8, 2 * cols))
    spectrum = dot(jnp.concatenate(turned[:-1] + [mine], 0), along[...])
    kx = wavenumbers(nodes, cols)
    for t in range(per):
        u = spectrum[t * nodes : (t + 1) * nodes]
        g = spectrum[(per + t) * nodes : (per + t + 1) * nodes]
        send[pl.ds(t, nodes, stride=SEND_B), :] = g[:, :cols] - kx * u[:, cols:]
        send[pl.ds(per + t, nodes, stride=SEND_B), :] = g[:, cols:] + kx * u[:, :cols]
    for part in range(2):
        send[pl.ds(2 * per + part, nodes, stride=SEND_B), :] = jnp.zeros((nodes, cols), F32)
        edge[part : part + 1, :] = spectrum[2 * per * nodes : 2 * per * nodes + 1, part * cols : (part + 1) * cols]


def eliminate(nodes, per, got, edge, wide, heavy, base, left, right, send, rhs, ratio):
    rows, cols = wide.shape
    steps = lax.axis_size("gy")
    rank_x, rank_y = lax.axis_index("gx"), lax.axis_index("gy")
    for part in range(2):
        for t in range(per):
            rhs[part, pl.ds(t * nodes, nodes), :] = got[pl.ds(part * per + t, nodes, stride=SEND_B), :]
    place = lax.broadcasted_iota(jnp.int32, (1, cols), 1)
    kx = signed_half(rank_x + nodes * place, nodes * cols)
    square = kx * kx + KZ * KZ
    top = heavy[rows - 1 : rows, :]
    above_last = jnp.where(rank_y == steps - 1, 0.0, top)
    below_first = jnp.where(rank_y == 0, 0.0, jnp.full((1, cols), STANDIN, F32))

    def above(j):
        return above_last if j == rows - 1 else heavy[j : j + 1, :]

    def below(j):
        return below_first if j == 0 else heavy[j - 1 : j, :]

    def diagonal(j):
        return above(j) + below(j) + square * wide[j : j + 1, :]

    half = rows // 2
    low = high = None
    for i in range(half):
        j, k = i, rows - 1 - i
        if i == 0:
            inv_l, inv_h = 1.0 / diagonal(j), 1.0 / diagonal(k)
            low = (rhs[0, j : j + 1, :] * inv_l, rhs[1, j : j + 1, :] * inv_l, inv_l)
            high = (rhs[0, k : k + 1, :] * inv_h, rhs[1, k : k + 1, :] * inv_h, inv_h)
        else:
            gl, gh = below(j), above(k)
            inv_l = 1.0 / (diagonal(j) - gl * gl * inv_l)
            inv_h = 1.0 / (diagonal(k) - gh * gh * inv_h)
            low = (
                (rhs[0, j : j + 1, :] + gl * low[0]) * inv_l,
                (rhs[1, j : j + 1, :] + gl * low[1]) * inv_l,
                gl * low[2] * inv_l,
            )
            high = (
                (rhs[0, k : k + 1, :] + gh * high[0]) * inv_h,
                (rhs[1, k : k + 1, :] + gh * high[1]) * inv_h,
                gh * high[2] * inv_h,
            )
        e_l, e_h = above(j) * inv_l, below(k) * inv_h
        if i < half - 1:
            ratio[j : j + 1, :] = e_l
            ratio[k : k + 1, :] = e_h
            for part in range(2):
                base[part, j : j + 1, :] = low[part]
                base[part, k : k + 1, :] = high[part]
            left[j : j + 1, :] = low[2]
            right[k : k + 1, :] = high[2]
    meet = 1.0 / (1.0 - e_l * e_h)
    down = [(low[0] + e_l * high[0]) * meet, (low[1] + e_l * high[1]) * meet, low[2] * meet, e_l * high[2] * meet]
    up = [high[0] + e_h * down[0], high[1] + e_h * down[1], e_h * down[2], high[2] + e_h * down[3]]
    for i in range(half):
        j, k = half - 1 - i, half + i
        if i > 0:
            e_l, e_h = ratio[j : j + 1, :], ratio[k : k + 1, :]
            down = [
                base[0, j : j + 1, :] + e_l * down[0],
                base[1, j : j + 1, :] + e_l * down[1],
                left[j : j + 1, :] + e_l * down[2],
                e_l * down[3],
            ]
            up = [
                base[0, k : k + 1, :] + e_h * up[0],
                base[1, k : k + 1, :] + e_h * up[1],
                e_h * up[2],
                right[k : k + 1, :] + e_h * up[3],
            ]
        for row, value in ((j, down), (k, up)):
            base[0, row : row + 1, :] = value[0]
            base[1, row : row + 1, :] = value[1]
            left[row : row + 1, :] = value[2]
            right[row : row + 1, :] = value[3]
    inv_top = 1.0 / top
    told = jnp.concatenate(
        [
            down[0],
            down[1],
            up[0] + edge[0:1, :] * inv_top,
            up[1] + edge[1:2, :] * inv_top,
            down[2],
            down[3],
            up[3],
            top,
        ],
        0,
    )
    for step in range(steps):
        send[8 * step : 8 * step + 8, :] = told


def couple(nodes, per, steps, got, base, left, right, send, chain):
    cols = left.shape[1]
    rank = lax.axis_index("gy")

    def told(block, i):
        return got[8 * block + i : 8 * block + i + 1, :]

    zero = jnp.zeros((1, cols), F32)
    g, offset, rho = zero, (zero, zero), zero
    for block in range(steps):
        a, b, c = told(block, 4), told(block, 5), told(block, 6)
        first = [told(block, 0), told(block, 1)]
        last = [told(block, 2), told(block, 3)]
        pushed = [g * offset[0], g * offset[1]]
        kappa = zero if block == 0 else g * (g * rho - 1.0) + STANDIN
        inv = 1.0 / (1.0 - a * kappa)
        start = [(first[i] + a * pushed[i]) * inv for i in range(2)]
        slope = b * inv
        for i, value in enumerate([start[0], start[1], slope, pushed[0], pushed[1], kappa]):
            chain[block, i : i + 1, :] = value
        offset = [last[i] + b * (pushed[i] + kappa * start[i]) for i in range(2)]
        rho = c + b * kappa * slope
        g = told(block, 7)
    value = (zero, zero)
    for block in reversed(range(steps)):
        g = zero if block == steps - 1 else told(block, 7)
        chain[block, 6:7, :] = value[0]
        chain[block, 7:8, :] = value[1]
        value = [chain[block, i : i + 1, :] + chain[block, 2:3, :] * (g * value[i]) for i in range(2)]
    mine = chain[rank]
    own = got[pl.ds(pl.multiple_of(8 * rank, 8), 8), :]
    g_above = jnp.where(rank == steps - 1, 0.0, own[7:8])
    for part in range(2):
        upper = g_above * mine[6 + part : 7 + part]
        here = mine[part : part + 1] + mine[2:3] * upper
        lower = mine[3 + part : 4 + part] + mine[5:6] * here
        for t in range(per):
            rows = pl.ds(t * nodes, nodes)
            solved = base[part, rows, :] + left[rows, :] * lower + right[rows, :] * upper
            send[pl.ds(part * per + t, nodes, stride=SEND_C), :] = solved
        send[pl.ds(2 * per + part, nodes, stride=SEND_C), :] = jnp.broadcast_to(
            mine[6 + part : 7 + part], (nodes, cols)
        )


def inverse(nodes, per, got, across, along, turn, send, edge, pick):
    cols = got.shape[1]
    rank = lax.axis_index("gx")

    def slot(s):
        return got[pl.ds(s, nodes, stride=SEND_C), :]

    kx = wavenumbers(nodes, cols)
    flow, plain = [], []
    for t in range(per):
        real, imag = slot(t), slot(per + t)
        flow.append(jnp.concatenate([-kx * imag, kx * real], 1))
        plain.append(jnp.concatenate([real, imag], 1))
    over = [jnp.concatenate([slot(2 * per), slot(2 * per + 1)], 1)]
    begun = dot(jnp.concatenate(flow + plain + over, 0), along[...])
    c, s = turn[0], turn[1]
    real, imag = [], []
    for i in range(2 * per + 1):
        a = begun[i * nodes : (i + 1) * nodes, :cols]
        b = begun[i * nodes : (i + 1) * nodes, cols:]
        real.append(a * c - b * s)
        imag.append(b * c + a * s)
    both = jnp.concatenate([jnp.concatenate(real, 1), jnp.concatenate(imag, 1)], 0)
    done = dot(across[...], both)
    for i in range(2):
        for part in range(2):
            for t in range(per):
                block = done[part * nodes : (part + 1) * nodes, (i * per + t) * cols : (i * per + t + 1) * cols]
                send[pl.ds((2 * i + part) * per + t, nodes, stride=SEND_D), :] = block
    for extra in range(4 * per, SEND_D):
        send[pl.ds(extra, nodes, stride=SEND_D), :] = jnp.zeros((nodes, cols), F32)
    pick[...] = done[:, 2 * per * cols :]
    for part in range(2):
        edge[part : part + 1, :] = pick[pl.ds(rank + part * nodes, 1), :]


def finish(nodes, per, steps, u, v, w, got, edge, heavy, u_new, v_new, w_new, pot):
    rows, cols = heavy.shape
    rank = lax.axis_index("gy")

    def slot(s):
        return got[pl.ds(s, nodes, stride=SEND_D), :]

    for part in range(2):
        for t in range(per):
            place = pl.ds(t * nodes, nodes)
            u_new[part, place, :] = u[part, place, :] - slot(part * per + t)
            pot[part, place, :] = slot((2 + part) * per + t)
    row = lax.broadcasted_iota(jnp.int32, (rows, cols), 0)
    g = jnp.where((row == rows - 1) & (rank == steps - 1), 0.0, heavy[...])
    for part in range(2):
        here = pot[part]
        after = jnp.where(row == rows - 1, jnp.broadcast_to(edge[part : part + 1, :], (rows, cols)), pltpu.roll(here, rows - 1, 0))
        v_new[part] = v[part] - g * (after - here)
        turned = KZ * pot[1 - part]
        w_new[part] = w[part] + (turned if part == 0 else -turned)


def call(body, outs, scratch, count, flops=1000000):
    return pl.pallas_call(
        body,
        out_shape=[jax.ShapeDtypeStruct(shape, F32) for shape in outs],
        in_specs=[VMEM] * count,
        out_specs=[VMEM] * len(outs),
        scratch_shapes=[pltpu.VMEM(shape, F32) for shape in scratch],
        compiler_params=pltpu.CompilerParams(vmem_limit_bytes=32 * 1024 * 1024),
        cost_estimate=pl.CostEstimate(flops=flops, bytes_accessed=1000000, transcendentals=0),
    )


def exchange(array, axis, count):
    shape = array.shape
    array = array.reshape(count, shape[0] // count, shape[1])
    return lax.all_to_all(array, axis, 0, 0, tiled=True).reshape(shape)


def per_device(u_star, v_star, w_star, cell_width, face_weight):
    nodes, steps = lax.axis_size("gx"), lax.axis_size("gy")
    shape = u_star.shape
    rows, cols = shape[2:]
    per = rows // nodes
    across_f, across_i, along_f, along_i, turn = tables(nodes, cols)
    u, v, w = (x.reshape(2, rows, cols) for x in (u_star, v_star, w_star))
    field, plane = (2, rows, cols), (rows, cols)

    send, wide, heavy = call(
        functools.partial(prepare, nodes), [(nodes * SEND_A, cols), plane, plane], [(4, rows, cols)], 5
    )(u, v, w, cell_width.reshape(1, rows), face_weight.reshape(1, rows))
    got = exchange(send, "gx", nodes)
    send, edge = call(
        functools.partial(forward, nodes, per), [(nodes * SEND_B, cols), (8, cols)], [(nodes, 2 * cols)], 4
    )(got, across_f, along_f, turn)
    got = exchange(send, "gx", nodes)
    base, left, right, send = call(
        functools.partial(eliminate, nodes, per), [field, plane, plane, (8 * steps, cols)], [field, plane], 4
    )(got, edge, wide, heavy)
    got = exchange(send, "gy", steps)
    (send,) = call(
        functools.partial(couple, nodes, per, steps), [(nodes * SEND_C, cols)], [(steps, 8, cols)], 4
    )(got, base, left, right)
    got = exchange(send, "gx", nodes)
    send, edge = call(
        functools.partial(inverse, nodes, per), [(nodes * SEND_D, cols), (8, cols)], [(2 * nodes, cols)], 4
    )(got, across_i, along_i, turn)
    got = exchange(send, "gx", nodes)
    outs = call(functools.partial(finish, nodes, per, steps), [field] * 3, [field], 6)(u, v, w, got, edge, heavy)
    return tuple(x.reshape(shape) for x in outs)


def solution(mesh):
    whole = P(None, None, "gy", "gx")
    return jax.shard_map(
        per_device,
        mesh=mesh,
        in_specs=(whole, whole, whole, P("gy"), P("gy")),
        out_specs=(whole, whole, whole),
        check_vma=False,
    )
```

time: 705 us -> 93 us (0.13)
  the two profiles are of different devices: /device:TPU:196 before, /device:TPU:8 now
where the time goes in v1:
time: 93 us; the launch traced here: 92.6 us
  blocking collectives  85 us (91%)
  Pallas kernels  3.51 us (4%)
  local copies, waits for them, and re-layouts  3.38 us (4%)
    all_to_all x5, blocking collectives, exchange(): return lax.all_to_all(array, axis, 0, 0, tiled=True).reshape(shape)  85 us
    unnamed x26, local copies, waits for them, and re-layouts  3.38 us

profile of v1, /device:TPU:8, one launch (start us, length us, event | category | flops | bytes accessed | tf_op | source)
XLA Modules:
  0.0 92.6 jit_solution(17579841885192077223)
XLA Ops:
  0.6 0.0 copy-start.11
  0.6 0.0 copy-start.12
  0.7 0.6 copy-done.11
  1.3 0.0 copy-done.12
  1.3 0.0 copy-start
  1.3 0.9 copy-done
  2.2 0.0 copy-start.2
  2.2 0.9 copy-done.2
  3.1 0.0 copy-start.4
  3.1 0.9 copy-done.4
  4.0 0.1 shard_map.121
  4.1 0.0 copy-start.7
  4.1 0.0 copy-start.8
  4.2 0.0 copy-start.10
  4.2 22.4 %all_to_all.25 = f32[32,16,128]{2,1,0:T(8,128)S(1)} all-to-all(f32[32,16,128]{2,1,0:T(8,128)S(1)} %bitcast.36), channel_id=1, replica_groups=mesh['gx'=32,'gy'=16] {'gx'}, dimensions={0} | all-to-all | bytes 524288 | tf_op jit(solution)/shard_map/all_to_all | solution.py:327
  26.6 0.0 copy-done.7
  26.6 0.0 copy-done.8
  26.6 0.0 copy-done.10
  26.6 0.7 shard_map.122
  27.2 14.0 %all_to_all.26 = f32[32,8,128]{2,1,0:T(8,128)S(1)} all-to-all(f32[32,8,128]{2,1,0:T(8,128)S(1)} %bitcast.38), channel_id=1, replica_groups=mesh['gx'=32,'gy'=16] {'gx'}, dimensions={0} | all-to-all | bytes 262144 | tf_op jit(solution)/shard_map/all_to_all | solution.py:327
  41.3 0.6 shard_map.123
  41.9 18.1 %all_to_all.27 = f32[16,8,128]{2,1,0:T(8,128)S(1)} all-to-all(f32[16,8,128]{2,1,0:T(8,128)S(1)} %bitcast.39), channel_id=1, replica_groups=mesh['gx'=32,'gy'=16] {'gy'}, dimensions={0} | all-to-all | bytes 131072 | tf_op jit(solution)/shard_map/all_to_all | solution.py:327
  60.0 0.0 copy-start.6
  60.0 0.3 shard_map.124
  60.3 0.0 copy-start.9
  60.3 14.4 %all_to_all.28 = f32[32,8,128]{2,1,0:T(8,128)S(1)} all-to-all(f32[32,8,128]{2,1,0:T(8,128)S(1)} %bitcast.27), channel_id=1, replica_groups=mesh['gx'=32,'gy'=16] {'gx'}, dimensions={0} | all-to-all | bytes 262144 | tf_op jit(solution)/shard_map/all_to_all | solution.py:327
  74.7 0.0 copy-done.6
  74.7 0.0 copy-done.9
  74.7 1.0 %shard_map.125 = (f32[512,128]{1,0:T(8,128)S(1)}, f32[8,128]{1,0:T(8,128)S(1)}) custom-call(f32[256,128]{1,0:T(8,128)S(1)} %bitcast.26, f32[64,64]{1,0:T(8,128)S(1)} %copy-done.9, f32[256,256]{1,0:T(8,128)S(1)} %copy-done.6, f32[2,32,128]{2,1,0:T(8,128)S(1)} %copy-done.8), custom_call_target="tpu_custom_call" | custom-call | flops 1000000 | bytes 1000000 | tf_op jit(solution)/shard_map/pallas_call | solution.py:355
  75.7 0.0 copy-start.1
  75.7 0.0 copy-start.3
  75.7 0.0 copy-start.5
  75.7 16.1 %all_to_all.29 = f32[32,16,128]{2,1,0:T(8,128)S(1)} all-to-all(f32[32,16,128]{2,1,0:T(8,128)S(1)} %bitcast.35), channel_id=1, replica_groups=mesh['gx'=32,'gy'=16] {'gx'}, dimensions={0} | all-to-all | bytes 524288 | tf_op jit(solution)/shard_map/all_to_all | solution.py:327
  91.8 0.0 copy-done.1
  91.8 0.0 copy-done.3
  91.8 0.0 copy-done.5
  91.8 0.8 shard_map.126
Async XLA Ops:
  0.6 0.7 copy-start.11
  0.6 0.7 copy-start.12
  1.3 0.9 copy-start
  2.2 0.9 copy-start.2
  3.1 0.9 copy-start.4
  4.1 22.4 %copy-start.7 = (f32[256,256]{1,0:T(8,128)S(1)}, f32[256,256]{1,0:T(8,128)}, u32[]{:S(2)}) copy-start(f32[256,256]{1,0:T(8,128)} %constant.11.clone.along) | copy-start | bytes 786436
  4.1 22.4 %copy-start.8 = (f32[2,32,128]{2,1,0:T(8,128)S(1)}, f32[2,32,128]{2,1,0:T(8,128)}, u32[]{:S(2)}) copy-start(f32[2,32,128]{2,1,0:T(8,128)} %constant.12.clone.turn) | copy-start | bytes 98308
  4.2 22.4 %copy-start.10 = (f32[64,64]{1,0:T(8,128)S(1)}, f32[64,64]{1,0:T(8,128)}, u32[]{:S(2)}) copy-start(f32[64,64]{1,0:T(8,128)} %constant.10.clone.across) | copy-start | bytes 49156
  60.0 14.7 %copy-start.6 = (f32[256,256]{1,0:T(8,128)S(1)}, f32[256,256]{1,0:T(8,128)}, u32[]{:S(2)}) copy-start(f32[256,256]{1,0:T(8,128)} %constant.14.clone.along) | copy-start | bytes 786436
  60.3 14.4 %copy-start.9 = (f32[64,64]{1,0:T(8,128)S(1)}, f32[64,64]{1,0:T(8,128)}, u32[]{:S(2)}) copy-start(f32[64,64]{1,0:T(8,128)} %constant.13.clone.across) | copy-start | bytes 49156
  75.7 16.1 %copy-start.1 = (f32[2,1,96,128]{3,2,1,0:T(8,128)S(1)}, f32[2,1,96,128]{3,2,1,0:T(8,128)}, u32[]{:S(2)}) copy-start(f32[2,1,96,128]{3,2,1,0:T(8,128)} %param.10) | copy-start | bytes 294916
  75.7 16.1 %copy-start.3 = (f32[2,1,96,128]{3,2,1,0:T(8,128)S(1)}, f32[2,1,96,128]{3,2,1,0:T(8,128)}, u32[]{:S(2)}) copy-start(f32[2,1,96,128]{3,2,1,0:T(8,128)} %param.11) | copy-start | bytes 294916
  75.7 16.1 %copy-start.5 = (f32[2,1,96,128]{3,2,1,0:T(8,128)S(1)}, f32[2,1,96,128]{3,2,1,0:T(8,128)}, u32[]{:S(2)}) copy-start(f32[2,1,96,128]{3,2,1,0:T(8,128)} %param.12) | copy-start | bytes 294916

commit v2 on v1

--- a/solution.py
+++ b/solution.py
@@ -16,7 +16,8 @@
 HIGHEST = lax.Precision.HIGHEST
 F32 = jnp.float32
 VMEM = pl.BlockSpec(memory_space=pltpu.VMEM)
-SEND_A, SEND_B, SEND_C, SEND_D = 16, 8, 8, 16
+HBM = pl.BlockSpec(memory_space=pltpu.HBM)
+SEND_A, SEND_B, SEND_C, SEND_D = 14, 6, 8, 12
 
 
 def tables(nodes, cols):
@@ -57,15 +58,29 @@
     return jnp.broadcast_to(one, (rows, cols))
 
 
-def prepare(nodes, u, v, w, width, weight, send, wide, heavy, tmp):
+def prepare(nodes, u_far, v_far, w_far, width_far, weight_far, send, wide, heavy, u, v, w, width, weight, tmp, arrived):
     rows, cols = u.shape[1:]
     per = rows // nodes
+    copies = [
+        pltpu.make_async_copy(far, near, arrived.at[i])
+        for i, (far, near) in enumerate(
+            ((width_far, width), (weight_far, weight), (u_far, u), (w_far, w), (v_far, v))
+        )
+    ]
+    for copy in copies:
+        copy.start()
+    copies[0].wait()
     h = column(width[...], rows, cols)
     wide[...] = h
+    copies[1].wait()
     heavy[...] = column(weight[...], rows, cols)
+    copies[2].wait()
+    for part in range(2):
+        tmp[part] = -h * u[part]
+    copies[3].wait()
+    copies[4].wait()
     first = lax.broadcasted_iota(jnp.int32, (rows, cols), 0) == 0
     for part in range(2):
-        tmp[part] = -h * u[part]
         now = v[part]
         below = jnp.where(first, 0.0, pltpu.roll(now, 1, 0))
         other = w[1 - part] * (h * KZ)
@@ -76,7 +91,6 @@
     for part in range(2):
         last = jnp.broadcast_to(v[part, rows - 1 : rows, :], (nodes, cols))
         send[pl.ds(4 * per + part, nodes, stride=SEND_A), :] = last
-        send[pl.ds(4 * per + 2 + part, nodes, stride=SEND_A), :] = jnp.zeros_like(last)
 
 
 def forward(nodes, per, got, across, along, turn, send, edge, pick):
@@ -106,7 +120,6 @@
         send[pl.ds(t, nodes, stride=SEND_B), :] = g[:, :cols] - kx * u[:, cols:]
         send[pl.ds(per + t, nodes, stride=SEND_B), :] = g[:, cols:] + kx * u[:, :cols]
     for part in range(2):
-        send[pl.ds(2 * per + part, nodes, stride=SEND_B), :] = jnp.zeros((nodes, cols), F32)
         edge[part : part + 1, :] = spectrum[2 * per * nodes : 2 * per * nodes + 1, part * cols : (part + 1) * cols]
 
 
@@ -280,16 +293,19 @@
             for t in range(per):
                 block = done[part * nodes : (part + 1) * nodes, (i * per + t) * cols : (i * per + t + 1) * cols]
                 send[pl.ds((2 * i + part) * per + t, nodes, stride=SEND_D), :] = block
-    for extra in range(4 * per, SEND_D):
-        send[pl.ds(extra, nodes, stride=SEND_D), :] = jnp.zeros((nodes, cols), F32)
     pick[...] = done[:, 2 * per * cols :]
     for part in range(2):
         edge[part : part + 1, :] = pick[pl.ds(rank + part * nodes, 1), :]
 
 
-def finish(nodes, per, steps, u, v, w, got, edge, heavy, u_new, v_new, w_new, pot):
+def finish(nodes, per, steps, u, v, w, got, edge, heavy, u_far, v_far, w_far, u_new, v_new, w_new, pot, left):
     rows, cols = heavy.shape
     rank = lax.axis_index("gy")
+    copies = [
+        pltpu.make_async_copy(near.at[part], far.at[part], left.at[2 * i + part])
+        for i, (near, far) in enumerate(((u_new, u_far), (w_new, w_far), (v_new, v_far)))
+        for part in range(2)
+    ]
 
     def slot(s):
         return got[pl.ds(s, nodes, stride=SEND_D), :]
@@ -298,32 +314,44 @@
         for t in range(per):
             place = pl.ds(t * nodes, nodes)
             u_new[part, place, :] = u[part, place, :] - slot(part * per + t)
-            pot[part, place, :] = slot((2 + part) * per + t)
+        copies[part].start()
+    for part in range(2):
+        for t in range(per):
+            pot[part, pl.ds(t * nodes, nodes), :] = slot((2 + part) * per + t)
+    for part in range(2):
+        turned = KZ * pot[1 - part]
+        w_new[part] = w[part] + (turned if part == 0 else -turned)
+        copies[2 + part].start()
     row = lax.broadcasted_iota(jnp.int32, (rows, cols), 0)
     g = jnp.where((row == rows - 1) & (rank == steps - 1), 0.0, heavy[...])
     for part in range(2):
         here = pot[part]
-        after = jnp.where(row == rows - 1, jnp.broadcast_to(edge[part : part + 1, :], (rows, cols)), pltpu.roll(here, rows - 1, 0))
+        above = jnp.broadcast_to(edge[part : part + 1, :], (rows, cols))
+        after = jnp.where(row == rows - 1, above, pltpu.roll(here, rows - 1, 0))
         v_new[part] = v[part] - g * (after - here)
-        turned = KZ * pot[1 - part]
-        w_new[part] = w[part] + (turned if part == 0 else -turned)
-
-
-def call(body, outs, scratch, count, flops=1000000):
+        copies[4 + part].start()
+    for copy in copies:
+        copy.wait()
+
+
+def call(body, outs, scratch, ins, out_spec=VMEM, semaphores=0, limit=24):
+    scratch = [pltpu.VMEM(shape, F32) for shape in scratch]
+    if semaphores:
+        scratch.append(pltpu.SemaphoreType.DMA((semaphores,)))
     return pl.pallas_call(
         body,
         out_shape=[jax.ShapeDtypeStruct(shape, F32) for shape in outs],
-        in_specs=[VMEM] * count,
-        out_specs=[VMEM] * len(outs),
-        scratch_shapes=[pltpu.VMEM(shape, F32) for shape in scratch],
-        compiler_params=pltpu.CompilerParams(vmem_limit_bytes=32 * 1024 * 1024),
-        cost_estimate=pl.CostEstimate(flops=flops, bytes_accessed=1000000, transcendentals=0),
+        in_specs=ins,
+        out_specs=[out_spec] * len(outs),
+        scratch_shapes=scratch,
+        compiler_params=pltpu.CompilerParams(vmem_limit_bytes=limit * 1024 * 1024),
+        cost_estimate=pl.CostEstimate(flops=1000000, bytes_accessed=1000000, transcendentals=0),
     )
 
 
 def exchange(array, axis, count):
     shape = array.shape
-    array = array.reshape(count, shape[0] // count, shape[1])
+    array = array.reshape(count, shape[0] // count * shape[1])
     return lax.all_to_all(array, axis, 0, 0, tiled=True).reshape(shape)
 
 
@@ -334,29 +362,44 @@
     per = rows // nodes
     across_f, across_i, along_f, along_i, turn = tables(nodes, cols)
     u, v, w = (x.reshape(2, rows, cols) for x in (u_star, v_star, w_star))
-    field, plane = (2, rows, cols), (rows, cols)
+    field, plane, line = (2, rows, cols), (rows, cols), (1, rows)
 
     send, wide, heavy = call(
-        functools.partial(prepare, nodes), [(nodes * SEND_A, cols), plane, plane], [(4, rows, cols)], 5
-    )(u, v, w, cell_width.reshape(1, rows), face_weight.reshape(1, rows))
+        functools.partial(prepare, nodes),
+        [(nodes * SEND_A, cols), plane, plane],
+        [field, field, field, line, line, (4, rows, cols)],
+        [HBM] * 5,
+        semaphores=5,
+        limit=60,
+    )(u, v, w, cell_width.reshape(line), face_weight.reshape(line))
     got = exchange(send, "gx", nodes)
     send, edge = call(
-        functools.partial(forward, nodes, per), [(nodes * SEND_B, cols), (8, cols)], [(nodes, 2 * cols)], 4
+        functools.partial(forward, nodes, per), [(nodes * SEND_B, cols), (8, cols)], [(nodes, 2 * cols)], [VMEM] * 4
     )(got, across_f, along_f, turn)
     got = exchange(send, "gx", nodes)
     base, left, right, send = call(
-        functools.partial(eliminate, nodes, per), [field, plane, plane, (8 * steps, cols)], [field, plane], 4
+        functools.partial(eliminate, nodes, per),
+        [field, plane, plane, (8 * steps, cols)],
+        [field, plane],
+        [VMEM] * 4,
     )(got, edge, wide, heavy)
     got = exchange(send, "gy", steps)
     (send,) = call(
-        functools.partial(couple, nodes, per, steps), [(nodes * SEND_C, cols)], [(steps, 8, cols)], 4
+        functools.partial(couple, nodes, per, steps), [(nodes * SEND_C, cols)], [(steps, 8, cols)], [VMEM] * 4
     )(got, base, left, right)
     got = exchange(send, "gx", nodes)
     send, edge = call(
-        functools.partial(inverse, nodes, per), [(nodes * SEND_D, cols), (8, cols)], [(2 * nodes, cols)], 4
+        functools.partial(inverse, nodes, per), [(nodes * SEND_D, cols), (8, cols)], [(2 * nodes, cols)], [VMEM] * 4
     )(got, across_i, along_i, turn)
     got = exchange(send, "gx", nodes)
-    outs = call(functools.partial(finish, nodes, per, steps), [field] * 3, [field], 6)(u, v, w, got, edge, heavy)
+    outs = call(
+        functools.partial(finish, nodes, per, steps),
+        [field] * 3,
+        [field] * 4,
+        [VMEM] * 6,
+        out_spec=HBM,
+        semaphores=6,
+    )(u, v, w, got, edge, heavy)
     return tuple(x.reshape(shape) for x in outs)
 
 

time: 93 us -> 89.3 us (0.960)
  local copies, waits for them, and re-layouts: 3.38 us -> 0.06 us
  blocking collectives: 85 us -> 83 us
  Pallas kernels: 3.51 us -> 5.09 us
    unnamed x26 -> x20, local copies, waits for them, and re-layouts: 3.38 us -> 0.06 us
    all_to_all x5, blocking collectives: 85 us -> 83 us  [exchange(): return lax.all_to_all(array, axis, 0, 0, tiled=True).reshape(shape)]
    pallas_call x1, Pallas kernels: 0.14 us -> 1.78 us  [per_device(): call(functools.partial(prepare, nodes), [(nodes * SEND_A, cols), plane, p...]
where the time goes in v2:
time: 89.3 us; the launch traced here: 88.9 us
  blocking collectives  83 us (93%)
  Pallas kernels  5.09 us (6%)
    all_to_all x5, blocking collectives, exchange(): return lax.all_to_all(array, axis, 0, 0, tiled=True).reshape(shape)  83 us

profile of v2, /device:TPU:8, one launch (start us, length us, event | category | flops | bytes accessed | tf_op | source)
XLA Modules:
  0.0 88.9 jit_solution(15970339181036145877)
XLA Ops:
  0.6 1.8 %shard_map.121 = (f32[448,128]{1,0:T(8,128)}, f32[96,128]{1,0:T(8,128)}, f32[96,128]{1,0:T(8,128)}) custom-call(f32[2,96,128]{2,1,0:T(8,128)} %bitcast.29, f32[2,96,128]{2,1,0:T(8,128)} %bitcast.31, f32[2,96,128]{2,1,0:T(8,128)} %bitcast.33, f32[1,96]{1,0:T(1,128)} %bitcast.40, f32[1,96]{1,0:T(1,128)} %bitcast.41), custom_call_target="tpu_custom_call" | custom-call | flops 1000000 | bytes 1000000 | tf_op jit(solution)/shard_map/pallas_call | solution.py:367
  2.4 0.0 copy-start.4
  2.4 0.0 copy-start.6
  2.4 0.0 copy-start.9
  2.5 21.9 %all_to_all.45 = f32[32,1,1792]{2,1,0:T(1,128)S(1)} all-to-all(f32[32,1,1792]{2,1,0:T(1,128)} %bitcast.39), channel_id=1, replica_groups=mesh['gx'=32,'gy'=16] {'gx'}, dimensions={0} | all-to-all | bytes 458752 | tf_op jit(solution)/shard_map/all_to_all | solution.py:355
  24.4 0.0 copy-done.4
  24.4 0.0 copy-done.6
  24.4 0.0 copy-done.9
  24.4 0.6 shard_map.122
  25.1 0.0 copy-start.5
  25.1 0.0 copy-start.7
  25.1 13.9 %all_to_all.46 = f32[32,1,768]{2,1,0:T(1,128)S(1)} all-to-all(f32[32,1,768]{2,1,0:T(1,128)S(1)} %bitcast.37), channel_id=1, replica_groups=mesh['gx'=32,'gy'=16] {'gx'}, dimensions={0} | all-to-all | bytes 196608 | tf_op jit(solution)/shard_map/all_to_all | solution.py:355
  39.0 0.0 copy-done.5
  39.0 0.0 copy-done.7
  39.0 0.6 shard_map.123
  39.6 18.1 %all_to_all.47 = f32[16,1,1024]{2,1,0:T(1,128)S(1)} all-to-all(f32[16,1,1024]{2,1,0:T(1,128)S(1)} %bitcast.38), channel_id=1, replica_groups=mesh['gx'=32,'gy'=16] {'gy'}, dimensions={0} | all-to-all | bytes 131072 | tf_op jit(solution)/shard_map/all_to_all | solution.py:355
  57.7 0.0 copy-start.3
  57.7 0.3 shard_map.124
  58.0 0.0 copy-start.8
  58.0 14.3 %all_to_all.48 = f32[32,1,1024]{2,1,0:T(1,128)S(1)} all-to-all(f32[32,1,1024]{2,1,0:T(1,128)S(1)} %bitcast.27), channel_id=1, replica_groups=mesh['gx'=32,'gy'=16] {'gx'}, dimensions={0} | all-to-all | bytes 262144 | tf_op jit(solution)/shard_map/all_to_all | solution.py:355
  72.3 0.0 copy-done.3
  72.3 0.0 copy-done.8
  72.3 1.0 %shard_map.125 = (f32[384,128]{1,0:T(8,128)S(1)}, f32[8,128]{1,0:T(8,128)S(1)}) custom-call(f32[256,128]{1,0:T(8,128)S(1)} %bitcast.26, f32[64,64]{1,0:T(8,128)S(1)} %copy-done.8, f32[256,256]{1,0:T(8,128)S(1)} %copy-done.3, f32[2,32,128]{2,1,0:T(8,128)S(1)} %copy-done.6), custom_call_target="tpu_custom_call" | custom-call | flops 1000000 | bytes 1000000 | tf_op jit(solution)/shard_map/pallas_call | solution.py:391
  73.3 0.0 copy-start
  73.3 0.0 copy-start.1
  73.3 0.0 copy-start.2
  73.3 14.8 %all_to_all.49 = f32[32,1,1536]{2,1,0:T(1,128)S(1)} all-to-all(f32[32,1,1536]{2,1,0:T(1,128)S(1)} %bitcast.36), channel_id=1, replica_groups=mesh['gx'=32,'gy'=16] {'gx'}, dimensions={0} | all-to-all | bytes 393216 | tf_op jit(solution)/shard_map/all_to_all | solution.py:355
  88.1 0.0 copy-done
  88.1 0.0 copy-done.1
  88.1 0.0 copy-done.2
  88.1 0.8 shard_map.126
Async XLA Ops:
  2.4 22.0 %copy-start.4 = (f32[256,256]{1,0:T(8,128)S(1)}, f32[256,256]{1,0:T(8,128)}, u32[]{:S(2)}) copy-start(f32[256,256]{1,0:T(8,128)} %constant.11.clone.along) | copy-start | bytes 786436
  2.4 22.0 %copy-start.6 = (f32[2,32,128]{2,1,0:T(8,128)S(1)}, f32[2,32,128]{2,1,0:T(8,128)}, u32[]{:S(2)}) copy-start(f32[2,32,128]{2,1,0:T(8,128)} %constant.12.clone.turn) | copy-start | bytes 98308
  2.4 22.0 %copy-start.9 = (f32[64,64]{1,0:T(8,128)S(1)}, f32[64,64]{1,0:T(8,128)}, u32[]{:S(2)}) copy-start(f32[64,64]{1,0:T(8,128)} %constant.10.clone.across) | copy-start | bytes 49156
  25.1 13.9 %copy-start.5 = (f32[96,128]{1,0:T(8,128)S(1)}, f32[96,128]{1,0:T(8,128)}, u32[]{:S(2)}) copy-start(f32[96,128]{1,0:T(8,128)} %get-tuple-element.21.heavy) | copy-start | bytes 147460
  25.1 13.9 %copy-start.7 = (f32[96,128]{1,0:T(8,128)S(1)}, f32[96,128]{1,0:T(8,128)}, u32[]{:S(2)}) copy-start(f32[96,128]{1,0:T(8,128)} %get-tuple-element.20.wide) | copy-start | bytes 147460
  57.7 14.6 %copy-start.3 = (f32[256,256]{1,0:T(8,128)S(1)}, f32[256,256]{1,0:T(8,128)}, u32[]{:S(2)}) copy-start(f32[256,256]{1,0:T(8,128)} %constant.14.clone.along) | copy-start | bytes 786436
  58.0 14.3 %copy-start.8 = (f32[64,64]{1,0:T(8,128)S(1)}, f32[64,64]{1,0:T(8,128)}, u32[]{:S(2)}) copy-start(f32[64,64]{1,0:T(8,128)} %constant.13.clone.across) | copy-start | bytes 49156
  73.3 14.8 %copy-start = (f32[2,1,96,128]{3,2,1,0:T(8,128)S(1)}, f32[2,1,96,128]{3,2,1,0:T(8,128)}, u32[]{:S(2)}) copy-start(f32[2,1,96,128]{3,2,1,0:T(8,128)} %param.10) | copy-start | bytes 294916
  73.3 14.8 %copy-start.1 = (f32[2,1,96,128]{3,2,1,0:T(8,128)S(1)}, f32[2,1,96,128]{3,2,1,0:T(8,128)}, u32[]{:S(2)}) copy-start(f32[2,1,96,128]{3,2,1,0:T(8,128)} %param.11) | copy-start | bytes 294916
  73.3 14.8 %copy-start.2 = (f32[2,1,96,128]{3,2,1,0:T(8,128)S(1)}, f32[2,1,96,128]{3,2,1,0:T(8,128)}, u32[]{:S(2)}) copy-start(f32[2,1,96,128]{3,2,1,0:T(8,128)} %param.12) | copy-start | bytes 294916

commit v3 on v2

--- a/solution.py
+++ b/solution.py
@@ -13,32 +13,54 @@
 SPAN_FACTOR = 1.0
 KZ = SPAN_FACTOR
 STANDIN = 16.0
-HIGHEST = lax.Precision.HIGHEST
+HIGH, HIGHEST = lax.Precision.HIGH, lax.Precision.HIGHEST
 F32 = jnp.float32
 VMEM = pl.BlockSpec(memory_space=pltpu.VMEM)
 HBM = pl.BlockSpec(memory_space=pltpu.HBM)
-SEND_A, SEND_B, SEND_C, SEND_D = 14, 6, 8, 12
+ALONG, BESIDE = 4, 4
+GROUP = ALONG * BESIDE
+SEND_C, SEND_D = 8, 12
+
+
+def order(nodes):
+    breadth = nodes // ALONG
+    return [
+        breadth * x + BESIDE * q + y for q in range(breadth // BESIDE) for y in range(BESIDE) for x in range(ALONG)
+    ]
+
+
+def place_of(nodes):
+    rank = lax.axis_index("gx")
+    x, y = rank // (nodes // ALONG), rank % (nodes // ALONG)
+    return y // BESIDE * GROUP + y % BESIDE * ALONG + x
 
 
 def tables(nodes, cols):
     full = nodes * cols
 
     def cos_sin(a, b, length):
-        angle = 2.0 * np.pi * (np.outer(np.arange(a), np.arange(b)) % length) / length
+        angle = 2.0 * np.pi * (np.outer(a, b) % length) / length
         return np.cos(angle), np.sin(angle)
 
-    c, s = cos_sin(nodes, nodes, nodes)
-    across_f = np.block([[c, s], [-s, c]])
+    ranks, residues, places = np.array(order(nodes)), np.arange(nodes), np.arange(cols)
+    c, s = cos_sin(residues, ranks, nodes)
+    across_f = np.stack(
+        [
+            np.block([[c[:, i : i + GROUP], s[:, i : i + GROUP]], [-s[:, i : i + GROUP], c[:, i : i + GROUP]]])
+            for i in range(0, nodes, GROUP)
+        ]
+    )
+    c, s = cos_sin(ranks, residues, nodes)
     across_i = np.block([[c, -s], [s, c]])
-    c, s = cos_sin(cols, cols, cols)
+    c, s = cos_sin(places, places, cols)
     along_f = np.block([[c, -s], [s, c]])
     along_i = np.block([[c, s], [-s, c]]) / full
-    turn = np.stack(cos_sin(nodes, cols, full))
+    turn = np.stack(cos_sin(residues, places, full))
     return [np.asarray(m, np.float32) for m in (across_f, across_i, along_f, along_i, turn)]
 
 
-def dot(a, b):
-    return lax.dot_general(a, b, (((1,), (0,)), ((), ())), precision=HIGHEST, preferred_element_type=F32)
+def dot(a, b, precision=HIGHEST):
+    return lax.dot_general(a, b, (((1,), (0,)), ((), ())), precision=precision, preferred_element_type=F32)
 
 
 def signed_half(wave, full):
@@ -58,9 +80,9 @@
     return jnp.broadcast_to(one, (rows, cols))
 
 
-def prepare(nodes, u_far, v_far, w_far, width_far, weight_far, send, wide, heavy, u, v, w, width, weight, tmp, arrived):
+def prepare(u_far, v_far, w_far, width_far, weight_far, send, wide, heavy, u, v, w, width, weight, tmp, arrived):
     rows, cols = u.shape[1:]
-    per = rows // nodes
+    per = rows // GROUP
     copies = [
         pltpu.make_async_copy(far, near, arrived.at[i])
         for i, (far, near) in enumerate(
@@ -85,51 +107,60 @@
         below = jnp.where(first, 0.0, pltpu.roll(now, 1, 0))
         other = w[1 - part] * (h * KZ)
         tmp[2 + part] = below - now + (other if part == 0 else -other)
+    to_each = 4 * per + 2
     for field in range(4):
         for t in range(per):
-            send[pl.ds(field * per + t, nodes, stride=SEND_A), :] = tmp[field, pl.ds(t * nodes, nodes), :]
-    for part in range(2):
-        last = jnp.broadcast_to(v[part, rows - 1 : rows, :], (nodes, cols))
-        send[pl.ds(4 * per + part, nodes, stride=SEND_A), :] = last
-
-
-def forward(nodes, per, got, across, along, turn, send, edge, pick):
+            send[pl.ds(field * per + t, GROUP, stride=to_each), :] = tmp[field, pl.ds(t * GROUP, GROUP), :]
+    for part in range(2):
+        last = jnp.broadcast_to(v[part, rows - 1 : rows, :], (GROUP, cols))
+        send[pl.ds(4 * per + part, GROUP, stride=to_each), :] = last
+
+
+def forward(nodes, got, across, along, turn, send):
     cols = got.shape[1]
-    rank = lax.axis_index("gx")
+    per = (got.shape[0] // GROUP - 2) // 4
+    group = place_of(nodes) // GROUP
 
     def slot(s):
-        return got[pl.ds(s, nodes, stride=SEND_A), :]
+        return got[pl.ds(s, GROUP, stride=4 * per + 2), :]
 
     real = [slot(t) for t in range(per)] + [slot(2 * per + t) for t in range(per)] + [slot(4 * per)]
     imag = [slot(per + t) for t in range(per)] + [slot(3 * per + t) for t in range(per)] + [slot(4 * per + 1)]
     both = jnp.concatenate([jnp.concatenate(real, 1), jnp.concatenate(imag, 1)], 0)
-    mixed = dot(across[...], both)
+    mixed = dot(across[group], both, HIGH)
     c, s = turn[0], turn[1]
     turned = []
     for i in range(2 * per + 1):
         a = mixed[:nodes, i * cols : (i + 1) * cols]
         b = mixed[nodes:, i * cols : (i + 1) * cols]
         turned.append(jnp.concatenate([a * c + b * s, b * c - a * s], 1))
-    pick[...] = turned[-1]
-    mine = jnp.broadcast_to(pick[pl.ds(rank, 1), :], (8, 2 * cols))
-    spectrum = dot(jnp.concatenate(turned[:-1] + [mine], 0), along[...])
+    spectrum = dot(jnp.concatenate(turned, 0), along[...], HIGH)
     kx = wavenumbers(nodes, cols)
+    to_each = 2 * per + 2
     for t in range(per):
         u = spectrum[t * nodes : (t + 1) * nodes]
         g = spectrum[(per + t) * nodes : (per + t + 1) * nodes]
-        send[pl.ds(t, nodes, stride=SEND_B), :] = g[:, :cols] - kx * u[:, cols:]
-        send[pl.ds(per + t, nodes, stride=SEND_B), :] = g[:, cols:] + kx * u[:, :cols]
-    for part in range(2):
-        edge[part : part + 1, :] = spectrum[2 * per * nodes : 2 * per * nodes + 1, part * cols : (part + 1) * cols]
-
-
-def eliminate(nodes, per, got, edge, wide, heavy, base, left, right, send, rhs, ratio):
+        send[pl.ds(t, nodes, stride=to_each), :] = g[:, :cols] - kx * u[:, cols:]
+        send[pl.ds(per + t, nodes, stride=to_each), :] = g[:, cols:] + kx * u[:, :cols]
+    last = spectrum[2 * per * nodes :]
+    for part in range(2):
+        send[pl.ds(2 * per + part, nodes, stride=to_each), :] = last[:, part * cols : (part + 1) * cols]
+
+
+def eliminate(nodes, got, wide, heavy, base, left, right, send, rhs, ratio):
     rows, cols = wide.shape
     steps = lax.axis_size("gy")
-    rank_x, rank_y = lax.axis_index("gx"), lax.axis_index("gy")
+    rank_x, rank_y = place_of(nodes), lax.axis_index("gy")
+    per = rows // GROUP
+    to_each = 2 * per + 2
+
+    def summed(s, count):
+        return sum(got[pl.ds(to_each * i + s, count, stride=to_each), :] for i in range(0, nodes, GROUP))
+
     for part in range(2):
         for t in range(per):
-            rhs[part, pl.ds(t * nodes, nodes), :] = got[pl.ds(part * per + t, nodes, stride=SEND_B), :]
+            rhs[part, pl.ds(t * GROUP, GROUP), :] = summed(part * per + t, GROUP)
+    edge = [summed(2 * per + part, 1) for part in range(2)]
     place = lax.broadcasted_iota(jnp.int32, (1, cols), 1)
     kx = signed_half(rank_x + nodes * place, nodes * cols)
     square = kx * kx + KZ * KZ
@@ -206,8 +237,8 @@
         [
             down[0],
             down[1],
-            up[0] + edge[0:1, :] * inv_top,
-            up[1] + edge[1:2, :] * inv_top,
+            up[0] + edge[0] * inv_top,
+            up[1] + edge[1] * inv_top,
             down[2],
             down[3],
             up[3],
@@ -266,10 +297,20 @@
 
 def inverse(nodes, per, got, across, along, turn, send, edge, pick):
     cols = got.shape[1]
-    rank = lax.axis_index("gx")
+    place = place_of(nodes)
 
     def slot(s):
         return got[pl.ds(s, nodes, stride=SEND_C), :]
+
+    def turned(begun):
+        c, s = turn[0], turn[1]
+        real, imag = [], []
+        for i in range(begun.shape[0] // nodes):
+            a = begun[i * nodes : (i + 1) * nodes, :cols]
+            b = begun[i * nodes : (i + 1) * nodes, cols:]
+            real.append(a * c - b * s)
+            imag.append(b * c + a * s)
+        return jnp.concatenate([jnp.concatenate(real, 1), jnp.concatenate(imag, 1)], 0)
 
     kx = wavenumbers(nodes, cols)
     flow, plain = [], []
@@ -277,25 +318,19 @@
         real, imag = slot(t), slot(per + t)
         flow.append(jnp.concatenate([-kx * imag, kx * real], 1))
         plain.append(jnp.concatenate([real, imag], 1))
-    over = [jnp.concatenate([slot(2 * per), slot(2 * per + 1)], 1)]
-    begun = dot(jnp.concatenate(flow + plain + over, 0), along[...])
-    c, s = turn[0], turn[1]
-    real, imag = [], []
-    for i in range(2 * per + 1):
-        a = begun[i * nodes : (i + 1) * nodes, :cols]
-        b = begun[i * nodes : (i + 1) * nodes, cols:]
-        real.append(a * c - b * s)
-        imag.append(b * c + a * s)
-    both = jnp.concatenate([jnp.concatenate(real, 1), jnp.concatenate(imag, 1)], 0)
-    done = dot(across[...], both)
-    for i in range(2):
+    plain.append(jnp.concatenate([slot(2 * per), slot(2 * per + 1)], 1))
+    plain = dot(jnp.concatenate(plain, 0), along[...])
+    flow = dot(jnp.concatenate(flow, 0), along[...], HIGH)
+    plain = dot(across[...], turned(plain))
+    flow = dot(across[...], turned(flow), HIGH)
+    for i, done in enumerate((flow, plain)):
         for part in range(2):
             for t in range(per):
-                block = done[part * nodes : (part + 1) * nodes, (i * per + t) * cols : (i * per + t + 1) * cols]
+                block = done[part * nodes : (part + 1) * nodes, t * cols : (t + 1) * cols]
                 send[pl.ds((2 * i + part) * per + t, nodes, stride=SEND_D), :] = block
-    pick[...] = done[:, 2 * per * cols :]
-    for part in range(2):
-        edge[part : part + 1, :] = pick[pl.ds(rank + part * nodes, 1), :]
+    pick[...] = plain[:, per * cols :]
+    for part in range(2):
+        edge[part : part + 1, :] = pick[pl.ds(place + part * nodes, 1), :]
 
 
 def finish(nodes, per, steps, u, v, w, got, edge, heavy, u_far, v_far, w_far, u_new, v_new, w_new, pot, left):
@@ -349,49 +384,51 @@
     )
 
 
-def exchange(array, axis, count):
+def exchange(array, axis, count, groups=None):
     shape = array.shape
     array = array.reshape(count, shape[0] // count * shape[1])
-    return lax.all_to_all(array, axis, 0, 0, tiled=True).reshape(shape)
+    return lax.all_to_all(array, axis, 0, 0, axis_index_groups=groups, tiled=True).reshape(shape)
 
 
 def per_device(u_star, v_star, w_star, cell_width, face_weight):
     nodes, steps = lax.axis_size("gx"), lax.axis_size("gy")
     shape = u_star.shape
     rows, cols = shape[2:]
-    per = rows // nodes
+    per, wider = rows // nodes, rows // GROUP
     across_f, across_i, along_f, along_i, turn = tables(nodes, cols)
     u, v, w = (x.reshape(2, rows, cols) for x in (u_star, v_star, w_star))
     field, plane, line = (2, rows, cols), (rows, cols), (1, rows)
+    ranks = order(nodes)
+    near, all_x = [ranks[i : i + GROUP] for i in range(0, nodes, GROUP)], [ranks]
 
     send, wide, heavy = call(
-        functools.partial(prepare, nodes),
-        [(nodes * SEND_A, cols), plane, plane],
+        prepare,
+        [(GROUP * (4 * wider + 2), cols), plane, plane],
         [field, field, field, line, line, (4, rows, cols)],
         [HBM] * 5,
         semaphores=5,
         limit=60,
     )(u, v, w, cell_width.reshape(line), face_weight.reshape(line))
-    got = exchange(send, "gx", nodes)
-    send, edge = call(
-        functools.partial(forward, nodes, per), [(nodes * SEND_B, cols), (8, cols)], [(nodes, 2 * cols)], [VMEM] * 4
-    )(got, across_f, along_f, turn)
-    got = exchange(send, "gx", nodes)
+    got = exchange(send, "gx", GROUP, near)
+    (send,) = call(functools.partial(forward, nodes), [(nodes * (2 * wider + 2), cols)], [], [VMEM] * 4)(
+        got, across_f, along_f, turn
+    )
+    got = exchange(send, "gx", nodes, all_x)
     base, left, right, send = call(
-        functools.partial(eliminate, nodes, per),
+        functools.partial(eliminate, nodes),
         [field, plane, plane, (8 * steps, cols)],
         [field, plane],
-        [VMEM] * 4,
-    )(got, edge, wide, heavy)
+        [VMEM] * 3,
+    )(got, wide, heavy)
     got = exchange(send, "gy", steps)
     (send,) = call(
         functools.partial(couple, nodes, per, steps), [(nodes * SEND_C, cols)], [(steps, 8, cols)], [VMEM] * 4
     )(got, base, left, right)
-    got = exchange(send, "gx", nodes)
+    got = exchange(send, "gx", nodes, all_x)
     send, edge = call(
         functools.partial(inverse, nodes, per), [(nodes * SEND_D, cols), (8, cols)], [(2 * nodes, cols)], [VMEM] * 4
     )(got, across_i, along_i, turn)
-    got = exchange(send, "gx", nodes)
+    got = exchange(send, "gx", nodes, all_x)
     outs = call(
         functools.partial(finish, nodes, per, steps),
         [field] * 3,

time: 89.3 us -> 86.4 us (0.968)
  blocking collectives: 83 us -> 80.4 us
    all_to_all x5, blocking collectives: 83 us -> 80.4 us  [exchange(): lax.all_to_all(array, axis, 0, 0, axis_index_groups=groups, tiled=True)]
where the time goes in v3:
time: 86.4 us; the launch traced here: 86 us
  blocking collectives  80.4 us (93%)
  Pallas kernels  4.81 us (6%)
    all_to_all x5, blocking collectives, exchange(): lax.all_to_all(array, axis, 0, 0, axis_index_groups=groups, tiled=True)  80.4 us
    pallas_call x1, Pallas kernels, per_device(): call(prepare, [(GROUP * (4 * wider + 2), cols), plane, plane], [field, fi...  1.79 us

profile of v3, /device:TPU:8, one launch (start us, length us, event | category | flops | bytes accessed | tf_op | source)
XLA Modules:
  0.0 86.0 jit_solution(6409860878283580826)
XLA Ops:
  0.6 1.8 %shard_map.121 = (f32[416,128]{1,0:T(8,128)}, f32[96,128]{1,0:T(8,128)}, f32[96,128]{1,0:T(8,128)}) custom-call(f32[2,96,128]{2,1,0:T(8,128)} %bitcast.30, f32[2,96,128]{2,1,0:T(8,128)} %bitcast.32, f32[2,96,128]{2,1,0:T(8,128)} %bitcast.34, f32[1,96]{1,0:T(1,128)} %bitcast.40, f32[1,96]{1,0:T(1,128)} %bitcast.41), custom_call_target="tpu_custom_call" | custom-call | flops 1000000 | bytes 1000000 | tf_op jit(solution)/shard_map/pallas_call | solution.py:404
  2.4 0.0 copy-start.3
  2.4 0.0 copy-start.6
  2.5 0.0 copy-start.7
  2.5 16.7 %all_to_all.45 = f32[16,1,3328]{2,1,0:T(1,128)S(1)} all-to-all(f32[16,1,3328]{2,1,0:T(1,128)} %bitcast.39), channel_id=1, replica_groups={{0,128,256,384,16,144,272,400,32,160,288,416,48,176,304,432},{64,192,32..., dimensions={0} | all-to-all | bytes 425984 | tf_op jit(solution)/shard_map/all_to_all | solution.py:390
  19.2 0.0 copy-done.3
  19.2 0.0 copy-done.6
  19.2 0.0 copy-done.7
  19.2 0.6 shard_map.122
  19.8 0.0 copy-start.5
  19.8 0.0 copy-start.8
  19.8 16.6 %all_to_all.46 = f32[32,1,1792]{2,1,0:T(1,128)S(1)} all-to-all(f32[32,1,1792]{2,1,0:T(1,128)S(1)} %bitcast.25), channel_id=1, replica_groups={{0,128,256,384,16,144,272,400,32,160,288,416,48,176,304,432,64,192,320,..., dimensions={0} | all-to-all | bytes 458752 | tf_op jit(solution)/shard_map/all_to_all | solution.py:390
  36.5 0.0 copy-done.5
  36.5 0.0 copy-done.8
  36.5 0.6 shard_map.123
  37.1 18.1 %all_to_all.47 = f32[16,1,1024]{2,1,0:T(1,128)S(1)} all-to-all(f32[16,1,1024]{2,1,0:T(1,128)S(1)} %bitcast.38), channel_id=1, replica_groups=mesh['gx'=32,'gy'=16] {'gy'}, dimensions={0} | all-to-all | bytes 131072 | tf_op jit(solution)/shard_map/all_to_all | solution.py:390
  55.2 0.0 copy-start.4
  55.2 0.3 shard_map.124
  55.5 0.0 copy-start.9
  55.5 14.4 %all_to_all.48 = f32[32,1,1024]{2,1,0:T(1,128)S(1)} all-to-all(f32[32,1,1024]{2,1,0:T(1,128)S(1)} %bitcast.29), channel_id=1, replica_groups={{0,128,256,384,16,144,272,400,32,160,288,416,48,176,304,432,64,192,320,..., dimensions={0} | all-to-all | bytes 262144 | tf_op jit(solution)/shard_map/all_to_all | solution.py:390
  70.0 0.0 copy-done.4
  70.0 0.0 copy-done.9
  70.0 0.7 shard_map.125
  70.7 0.0 copy-start
  70.7 0.0 copy-start.1
  70.7 0.0 copy-start.2
  70.7 14.5 %all_to_all.49 = f32[32,1,1536]{2,1,0:T(1,128)S(1)} all-to-all(f32[32,1,1536]{2,1,0:T(1,128)S(1)} %bitcast.37), channel_id=1, replica_groups={{0,128,256,384,16,144,272,400,32,160,288,416,48,176,304,432,64,192,320,..., dimensions={0} | all-to-all | bytes 393216 | tf_op jit(solution)/shard_map/all_to_all | solution.py:390
  85.2 0.0 copy-done
  85.2 0.0 copy-done.1
  85.2 0.0 copy-done.2
  85.2 0.8 shard_map.126
Async XLA Ops:
  2.4 16.8 %copy-start.3 = (f32[256,256]{1,0:T(8,128)S(1)}, f32[256,256]{1,0:T(8,128)}, u32[]{:S(2)}) copy-start(f32[256,256]{1,0:T(8,128)} %constant.11.clone.along) | copy-start | bytes 786436
  2.4 16.7 %copy-start.6 = (f32[2,32,128]{2,1,0:T(8,128)S(1)}, f32[2,32,128]{2,1,0:T(8,128)}, u32[]{:S(2)}) copy-start(f32[2,32,128]{2,1,0:T(8,128)} %constant.12.clone.turn) | copy-start | bytes 98308
  2.5 16.7 %copy-start.7 = (f32[2,64,32]{2,1,0:T(8,128)S(1)}, f32[2,64,32]{2,1,0:T(8,128)}, u32[]{:S(2)}) copy-start(f32[2,64,32]{2,1,0:T(8,128)} %constant.10.clone.across) | copy-start | bytes 49156
  19.8 16.6 %copy-start.5 = (f32[96,128]{1,0:T(8,128)S(1)}, f32[96,128]{1,0:T(8,128)}, u32[]{:S(2)}) copy-start(f32[96,128]{1,0:T(8,128)} %get-tuple-element.17.heavy) | copy-start | bytes 147460
  19.8 16.6 %copy-start.8 = (f32[96,128]{1,0:T(8,128)S(1)}, f32[96,128]{1,0:T(8,128)}, u32[]{:S(2)}) copy-start(f32[96,128]{1,0:T(8,128)} %get-tuple-element.16.wide) | copy-start | bytes 147460
  55.2 14.8 %copy-start.4 = (f32[256,256]{1,0:T(8,128)S(1)}, f32[256,256]{1,0:T(8,128)}, u32[]{:S(2)}) copy-start(f32[256,256]{1,0:T(8,128)} %constant.14.clone.along) | copy-start | bytes 786436
  55.5 14.5 %copy-start.9 = (f32[64,64]{1,0:T(8,128)S(1)}, f32[64,64]{1,0:T(8,128)}, u32[]{:S(2)}) copy-start(f32[64,64]{1,0:T(8,128)} %constant.13.clone.across) | copy-start | bytes 49156
  70.7 14.5 %copy-start = (f32[2,1,96,128]{3,2,1,0:T(8,128)S(1)}, f32[2,1,96,128]{3,2,1,0:T(8,128)}, u32[]{:S(2)}) copy-start(f32[2,1,96,128]{3,2,1,0:T(8,128)} %param.10) | copy-start | bytes 294916
  70.7 14.5 %copy-start.1 = (f32[2,1,96,128]{3,2,1,0:T(8,128)S(1)}, f32[2,1,96,128]{3,2,1,0:T(8,128)}, u32[]{:S(2)}) copy-start(f32[2,1,96,128]{3,2,1,0:T(8,128)} %param.11) | copy-start | bytes 294916
  70.7 14.5 %copy-start.2 = (f32[2,1,96,128]{3,2,1,0:T(8,128)S(1)}, f32[2,1,96,128]{3,2,1,0:T(8,128)}, u32[]{:S(2)}) copy-start(f32[2,1,96,128]{3,2,1,0:T(8,128)} %param.12) | copy-start | bytes 294916

commit v4 on v3

--- a/solution.py
+++ b/solution.py
@@ -407,8 +407,7 @@
         [field, field, field, line, line, (4, rows, cols)],
         [HBM] * 5,
         semaphores=5,
-        limit=60,
-    )(u, v, w, cell_width.reshape(line), face_weight.reshape(line))
+    )(*(pltpu.with_memory_space_constraint(x, pltpu.HBM) for x in (u, v, w, cell_width.reshape(line), face_weight.reshape(line))))
     got = exchange(send, "gx", GROUP, near)
     (send,) = call(functools.partial(forward, nodes), [(nodes * (2 * wider + 2), cols)], [], [VMEM] * 4)(
         got, across_f, along_f, turn

time: 86.4 us -> 85.2 us (0.986)
  no operation moved by 1% of the time
where the time goes in v4:
time: 85.2 us; the launch traced here: 84.9 us
  blocking collectives  80 us (94%)
  Pallas kernels  4.08 us (5%)
    all_to_all x5, blocking collectives, exchange(): lax.all_to_all(array, axis, 0, 0, axis_index_groups=groups, tiled=True)  80 us

profile of v4, /device:TPU:8, one launch (start us, length us, event | category | flops | bytes accessed | tf_op | source)
XLA Modules:
  0.0 84.9 jit_solution(17647096087139697382)
XLA Ops:
  0.6 1.1 %shard_map.121 = (f32[416,128]{1,0:T(8,128)S(1)}, f32[96,128]{1,0:T(8,128)S(1)}, f32[96,128]{1,0:T(8,128)S(1)}) custom-call(f32[2,96,128]{2,1,0:T(8,128)} %bitcast.30, f32[2,96,128]{2,1,0:T(8,128)} %bitcast.32, f32[2,96,128]{2,1,0:T(8,128)} %bitcast.34, f32[1,96]{1,0:T(1,128)} %bitcast.40, f32[1,96]{1,0:T(1,128)} %bitcast.41), custom_call_target="tpu_custom_call" | custom-call | flops 1000000 | bytes 1000000 | tf_op jit(solution)/shard_map/pallas_call | solution.py:404
  1.7 0.0 copy-start.3
  1.7 0.0 copy-start.5
  1.8 0.0 copy-start.6
  1.8 15.8 %all_to_all.45 = f32[16,1,3328]{2,1,0:T(1,128)S(1)} all-to-all(f32[16,1,3328]{2,1,0:T(1,128)S(1)} %bitcast.37), channel_id=1, replica_groups={{0,128,256,384,16,144,272,400,32,160,288,416,48,176,304,432},{64,192,32..., dimensions={0} | all-to-all | bytes 425984 | tf_op jit(solution)/shard_map/all_to_all | solution.py:390
  17.6 0.0 copy-done.3
  17.6 0.0 copy-done.5
  17.6 0.0 copy-done.6
  17.6 0.6 shard_map.122
  18.2 17.2 %all_to_all.46 = f32[32,1,1792]{2,1,0:T(1,128)S(1)} all-to-all(f32[32,1,1792]{2,1,0:T(1,128)S(1)} %bitcast.25), channel_id=1, replica_groups={{0,128,256,384,16,144,272,400,32,160,288,416,48,176,304,432,64,192,320,..., dimensions={0} | all-to-all | bytes 458752 | tf_op jit(solution)/shard_map/all_to_all | solution.py:390
  35.4 0.6 shard_map.123
  36.0 18.1 %all_to_all.47 = f32[16,1,1024]{2,1,0:T(1,128)S(1)} all-to-all(f32[16,1,1024]{2,1,0:T(1,128)S(1)} %bitcast.39), channel_id=1, replica_groups=mesh['gx'=32,'gy'=16] {'gy'}, dimensions={0} | all-to-all | bytes 131072 | tf_op jit(solution)/shard_map/all_to_all | solution.py:390
  54.1 0.0 copy-start.4
  54.1 0.3 shard_map.124
  54.4 0.0 copy-start.7
  54.4 14.4 %all_to_all.48 = f32[32,1,1024]{2,1,0:T(1,128)S(1)} all-to-all(f32[32,1,1024]{2,1,0:T(1,128)S(1)} %bitcast.29), channel_id=1, replica_groups={{0,128,256,384,16,144,272,400,32,160,288,416,48,176,304,432,64,192,320,..., dimensions={0} | all-to-all | bytes 262144 | tf_op jit(solution)/shard_map/all_to_all | solution.py:390
  68.9 0.0 copy-done.4
  68.9 0.0 copy-done.7
  68.9 0.7 shard_map.125
  69.6 0.0 copy-start
  69.6 0.0 copy-start.1
  69.6 0.0 copy-start.2
  69.6 14.5 %all_to_all.49 = f32[32,1,1536]{2,1,0:T(1,128)S(1)} all-to-all(f32[32,1,1536]{2,1,0:T(1,128)S(1)} %bitcast.38), channel_id=1, replica_groups={{0,128,256,384,16,144,272,400,32,160,288,416,48,176,304,432,64,192,320,..., dimensions={0} | all-to-all | bytes 393216 | tf_op jit(solution)/shard_map/all_to_all | solution.py:390
  84.1 0.0 copy-done
  84.1 0.0 copy-done.1
  84.1 0.0 copy-done.2
  84.1 0.8 shard_map.126
Async XLA Ops:
  1.7 15.9 %copy-start.3 = (f32[256,256]{1,0:T(8,128)S(1)}, f32[256,256]{1,0:T(8,128)}, u32[]{:S(2)}) copy-start(f32[256,256]{1,0:T(8,128)} %constant.11.clone.along) | copy-start | bytes 786436
  1.7 15.8 %copy-start.5 = (f32[2,32,128]{2,1,0:T(8,128)S(1)}, f32[2,32,128]{2,1,0:T(8,128)}, u32[]{:S(2)}) copy-start(f32[2,32,128]{2,1,0:T(8,128)} %constant.12.clone.turn) | copy-start | bytes 98308
  1.8 15.8 %copy-start.6 = (f32[2,64,32]{2,1,0:T(8,128)S(1)}, f32[2,64,32]{2,1,0:T(8,128)}, u32[]{:S(2)}) copy-start(f32[2,64,32]{2,1,0:T(8,128)} %constant.10.clone.across) | copy-start | bytes 49156
  54.1 14.8 %copy-start.4 = (f32[256,256]{1,0:T(8,128)S(1)}, f32[256,256]{1,0:T(8,128)}, u32[]{:S(2)}) copy-start(f32[256,256]{1,0:T(8,128)} %constant.14.clone.along) | copy-start | bytes 786436
  54.4 14.5 %copy-start.7 = (f32[64,64]{1,0:T(8,128)S(1)}, f32[64,64]{1,0:T(8,128)}, u32[]{:S(2)}) copy-start(f32[64,64]{1,0:T(8,128)} %constant.13.clone.across) | copy-start | bytes 49156
  69.6 14.5 %copy-start = (f32[2,1,96,128]{3,2,1,0:T(8,128)S(1)}, f32[2,1,96,128]{3,2,1,0:T(8,128)}, u32[]{:S(2)}) copy-start(f32[2,1,96,128]{3,2,1,0:T(8,128)} %param.10) | copy-start | bytes 294916
  69.6 14.5 %copy-start.1 = (f32[2,1,96,128]{3,2,1,0:T(8,128)S(1)}, f32[2,1,96,128]{3,2,1,0:T(8,128)}, u32[]{:S(2)}) copy-start(f32[2,1,96,128]{3,2,1,0:T(8,128)} %param.11) | copy-start | bytes 294916
  69.6 14.5 %copy-start.2 = (f32[2,1,96,128]{3,2,1,0:T(8,128)S(1)}, f32[2,1,96,128]{3,2,1,0:T(8,128)}, u32[]{:S(2)}) copy-start(f32[2,1,96,128]{3,2,1,0:T(8,128)} %param.12) | copy-start | bytes 294916

commit v5 on v4

--- a/solution.py
+++ b/solution.py
@@ -13,12 +13,13 @@
 SPAN_FACTOR = 1.0
 KZ = SPAN_FACTOR
 STANDIN = 16.0
-HIGH, HIGHEST = lax.Precision.HIGH, lax.Precision.HIGHEST
 F32 = jnp.float32
 VMEM = pl.BlockSpec(memory_space=pltpu.VMEM)
 HBM = pl.BlockSpec(memory_space=pltpu.HBM)
 ALONG, BESIDE = 4, 4
 GROUP = ALONG * BESIDE
+LEVELS = 3
+SEGMENTS = 2**LEVELS
 SEND_C, SEND_D = 8, 12
 
 
@@ -56,11 +57,49 @@
     along_f = np.block([[c, -s], [s, c]])
     along_i = np.block([[c, s], [-s, c]]) / full
     turn = np.stack(cos_sin(residues, places, full))
-    return [np.asarray(m, np.float32) for m in (across_f, across_i, along_f, along_i, turn)]
-
-
-def dot(a, b, precision=HIGHEST):
-    return lax.dot_general(a, b, (((1,), (0,)), ((), ())), precision=precision, preferred_element_type=F32)
+    return [
+        constant_side(across_f, -1, 2),
+        constant_side(across_i, -1, 2),
+        constant_side(across_i, -1, 3),
+        constant_side(along_f, 0, 2),
+        constant_side(along_i, 0, 2),
+        constant_side(along_i, 0, 3),
+        np.asarray(turn, np.float32),
+    ]
+
+
+def pairs(terms):
+    return [(i, j) for i in range(terms) for j in range(terms) if i + j < terms]
+
+
+def expand(value, terms, one, whole):
+    parts = []
+    for _ in range(terms):
+        parts.append(value.astype(one))
+        value = value - parts[-1].astype(whole)
+    return parts
+
+
+def constant_side(matrix, axis, terms):
+    parts = expand(np.asarray(matrix, np.float64), terms, jnp.bfloat16, np.float64)
+    return np.concatenate([parts[i] for i, _ in pairs(terms)], axis)
+
+
+def data_side(value, axis, terms):
+    parts = expand(value, terms, jnp.bfloat16, F32)
+    return jnp.concatenate([parts[j] for _, j in pairs(terms)], axis)
+
+
+def dot(a, b):
+    return lax.dot_general(a, b, (((1,), (0,)), ((), ())), preferred_element_type=F32)
+
+
+def left_dot(constant, value, terms):
+    return dot(constant, data_side(value, 0, terms))
+
+
+def right_dot(value, constant, terms):
+    return dot(data_side(value, 1, terms), constant)
 
 
 def signed_half(wave, full):
@@ -127,14 +166,14 @@
     real = [slot(t) for t in range(per)] + [slot(2 * per + t) for t in range(per)] + [slot(4 * per)]
     imag = [slot(per + t) for t in range(per)] + [slot(3 * per + t) for t in range(per)] + [slot(4 * per + 1)]
     both = jnp.concatenate([jnp.concatenate(real, 1), jnp.concatenate(imag, 1)], 0)
-    mixed = dot(across[group], both, HIGH)
+    mixed = left_dot(across[group], both, 2)
     c, s = turn[0], turn[1]
     turned = []
     for i in range(2 * per + 1):
         a = mixed[:nodes, i * cols : (i + 1) * cols]
         b = mixed[nodes:, i * cols : (i + 1) * cols]
         turned.append(jnp.concatenate([a * c + b * s, b * c - a * s], 1))
-    spectrum = dot(jnp.concatenate(turned, 0), along[...], HIGH)
+    spectrum = right_dot(jnp.concatenate(turned, 0), along[...], 2)
     kx = wavenumbers(nodes, cols)
     to_each = 2 * per + 2
     for t in range(per):
@@ -147,8 +186,44 @@
         send[pl.ds(2 * per + part, nodes, stride=to_each), :] = last[:, part * cols : (part + 1) * cols]
 
 
-def eliminate(nodes, got, wide, heavy, base, left, right, send, rhs, ratio):
+def joined(first, last, a, b, c, gap):
+    count, joins, span = a.shape[0], [], 1
+    while span < count:
+
+        def ahead(value, by):
+            return pltpu.roll(value, count - by, 0) if by else value
+
+        g = ahead(gap, span - 1)
+        next_first, next_last = [ahead(x, span) for x in first], [ahead(x, span) for x in last]
+        next_a, next_b, next_c = ahead(a, span), ahead(b, span), ahead(c, span)
+        weight = g / (1.0 - g * g * c * next_a)
+        by_l, by_r = b * weight, next_b * weight
+        from_below = [(last[n] + c * g * next_first[n]) * weight for n in range(2)]
+        from_above = [(next_first[n] + next_a * g * last[n]) * weight for n in range(2)]
+        below_r, above_l = c * g * by_r, next_a * g * by_l
+        joins.append(from_below + from_above + [by_l, below_r, above_l, by_r])
+        first = [first[n] + b * from_above[n] for n in range(2)]
+        last = [next_last[n] + next_b * from_below[n] for n in range(2)]
+        a, b, c = a + b * above_l, b * by_r, next_c + next_b * below_r
+        span *= 2
+    return (first, last, a, b, c), joins
+
+
+def parted(joins, part, lower, upper):
+    run = lax.broadcasted_iota(jnp.int32, lower.shape, 0)
+    for level in reversed(range(len(joins))):
+        join, span = joins[level], 2**level
+        later = run // span % 2 == 1
+        from_below = join[part] + join[4] * lower + join[5] * upper
+        from_above = join[2 + part] + join[6] * lower + join[7] * upper
+        lower = jnp.where(later, pltpu.roll(from_below, span, 0), lower)
+        upper = jnp.where(later, pltpu.roll(upper, span, 0), from_above)
+    return lower, upper
+
+
+def eliminate(nodes, got, wide, heavy, base, left, right, tree, send, rhs):
     rows, cols = wide.shape
+    length = rows // SEGMENTS
     steps = lax.axis_size("gy")
     rank_x, rank_y = place_of(nodes), lax.axis_index("gy")
     per = rows // GROUP
@@ -161,141 +236,96 @@
         for t in range(per):
             rhs[part, pl.ds(t * GROUP, GROUP), :] = summed(part * per + t, GROUP)
     edge = [summed(2 * per + part, 1) for part in range(2)]
-    place = lax.broadcasted_iota(jnp.int32, (1, cols), 1)
+    place = lax.broadcasted_iota(jnp.int32, (SEGMENTS, cols), 1)
+    run = lax.broadcasted_iota(jnp.int32, (SEGMENTS, cols), 0)
     kx = signed_half(rank_x + nodes * place, nodes * cols)
     square = kx * kx + KZ * KZ
     top = heavy[rows - 1 : rows, :]
-    above_last = jnp.where(rank_y == steps - 1, 0.0, top)
-    below_first = jnp.where(rank_y == 0, 0.0, jnp.full((1, cols), STANDIN, F32))
-
-    def above(j):
-        return above_last if j == rows - 1 else heavy[j : j + 1, :]
-
-    def below(j):
-        return below_first if j == 0 else heavy[j - 1 : j, :]
-
-    def diagonal(j):
-        return above(j) + below(j) + square * wide[j : j + 1, :]
-
-    half = rows // 2
-    low = high = None
+    every = [pl.ds(t, SEGMENTS, stride=length) for t in range(length)]
+    above = [heavy[rows_t, :] for rows_t in every]
+    below = [jnp.where(run == 0, jnp.where(rank_y == 0, 0.0, STANDIN), pltpu.roll(above[-1], 1, 0))] + above[:-1]
+    above[-1] = jnp.where((run == SEGMENTS - 1) & (rank_y == steps - 1), 0.0, above[-1])
+    diagonal = [above[t] + below[t] + square * wide[every[t], :] for t in range(length)]
+    right_side = [[rhs[part, rows_t, :] for part in range(2)] for rows_t in every]
+
+    half = length // 2
+    low, high, ratio_l, ratio_h = [], [], [], []
     for i in range(half):
-        j, k = i, rows - 1 - i
+        j, k = i, length - 1 - i
         if i == 0:
-            inv_l, inv_h = 1.0 / diagonal(j), 1.0 / diagonal(k)
-            low = (rhs[0, j : j + 1, :] * inv_l, rhs[1, j : j + 1, :] * inv_l, inv_l)
-            high = (rhs[0, k : k + 1, :] * inv_h, rhs[1, k : k + 1, :] * inv_h, inv_h)
+            inv_l, inv_h = 1.0 / diagonal[j], 1.0 / diagonal[k]
+            low.append([right_side[j][0] * inv_l, right_side[j][1] * inv_l, inv_l])
+            high.append([right_side[k][0] * inv_h, right_side[k][1] * inv_h, inv_h])
         else:
-            gl, gh = below(j), above(k)
-            inv_l = 1.0 / (diagonal(j) - gl * gl * inv_l)
-            inv_h = 1.0 / (diagonal(k) - gh * gh * inv_h)
-            low = (
-                (rhs[0, j : j + 1, :] + gl * low[0]) * inv_l,
-                (rhs[1, j : j + 1, :] + gl * low[1]) * inv_l,
-                gl * low[2] * inv_l,
-            )
-            high = (
-                (rhs[0, k : k + 1, :] + gh * high[0]) * inv_h,
-                (rhs[1, k : k + 1, :] + gh * high[1]) * inv_h,
-                gh * high[2] * inv_h,
-            )
-        e_l, e_h = above(j) * inv_l, below(k) * inv_h
+            gl, gh = below[j], above[k]
+            inv_l = 1.0 / (diagonal[j] - gl * gl * inv_l)
+            inv_h = 1.0 / (diagonal[k] - gh * gh * inv_h)
+            was_l, was_h = low[-1], high[-1]
+            low.append([(right_side[j][n] + gl * was_l[n]) * inv_l for n in range(2)] + [gl * was_l[2] * inv_l])
+            high.append([(right_side[k][n] + gh * was_h[n]) * inv_h for n in range(2)] + [gh * was_h[2] * inv_h])
+        ratio_l.append(above[j] * inv_l)
+        ratio_h.append(below[k] * inv_h)
+    e_l, e_h = ratio_l[-1], ratio_h[-1]
+    meet = 1.0 / (1.0 - e_l * e_h)
+    down = [(low[-1][n] + e_l * high[-1][n]) * meet for n in range(2)] + [low[-1][2] * meet, e_l * high[-1][2] * meet]
+    up = [high[-1][n] + e_h * down[n] for n in range(2)] + [e_h * down[2], high[-1][2] + e_h * down[3]]
+    for i in reversed(range(half)):
+        j, k = i, length - 1 - i
         if i < half - 1:
-            ratio[j : j + 1, :] = e_l
-            ratio[k : k + 1, :] = e_h
-            for part in range(2):
-                base[part, j : j + 1, :] = low[part]
-                base[part, k : k + 1, :] = high[part]
-            left[j : j + 1, :] = low[2]
-            right[k : k + 1, :] = high[2]
-    meet = 1.0 / (1.0 - e_l * e_h)
-    down = [(low[0] + e_l * high[0]) * meet, (low[1] + e_l * high[1]) * meet, low[2] * meet, e_l * high[2] * meet]
-    up = [high[0] + e_h * down[0], high[1] + e_h * down[1], e_h * down[2], high[2] + e_h * down[3]]
-    for i in range(half):
-        j, k = half - 1 - i, half + i
-        if i > 0:
-            e_l, e_h = ratio[j : j + 1, :], ratio[k : k + 1, :]
-            down = [
-                base[0, j : j + 1, :] + e_l * down[0],
-                base[1, j : j + 1, :] + e_l * down[1],
-                left[j : j + 1, :] + e_l * down[2],
-                e_l * down[3],
-            ]
-            up = [
-                base[0, k : k + 1, :] + e_h * up[0],
-                base[1, k : k + 1, :] + e_h * up[1],
-                e_h * up[2],
-                right[k : k + 1, :] + e_h * up[3],
-            ]
-        for row, value in ((j, down), (k, up)):
-            base[0, row : row + 1, :] = value[0]
-            base[1, row : row + 1, :] = value[1]
-            left[row : row + 1, :] = value[2]
-            right[row : row + 1, :] = value[3]
+            e_l, e_h = ratio_l[i], ratio_h[i]
+            down = [low[i][n] + e_l * down[n] for n in range(3)] + [e_l * down[3]]
+            up = [high[i][n] + e_h * up[n] for n in range(2)] + [e_h * up[2], high[i][2] + e_h * up[3]]
+        for t, value in ((j, down), (k, up)):
+            here = pl.ds(t * SEGMENTS, SEGMENTS)
+            base[0, here, :], base[1, here, :], left[here, :], right[here, :] = value
+
+    (first, last, a, b, c), joins = joined(down[:2], up[:2], down[2], down[3], up[3], above[-1])
+    for level, join in enumerate(joins):
+        for i, value in enumerate(join):
+            tree[level, i] = value
     inv_top = 1.0 / top
-    told = jnp.concatenate(
-        [
-            down[0],
-            down[1],
-            up[0] + edge[0] * inv_top,
-            up[1] + edge[1] * inv_top,
-            down[2],
-            down[3],
-            up[3],
-            top,
-        ],
-        0,
-    )
+    told = [x[:1] for x in first + last + [a, b, c]] + [top]
+    for part in range(2):
+        told[2 + part] = told[2 + part] + edge[part] * inv_top
+    told = jnp.concatenate(told, 0)
     for step in range(steps):
         send[8 * step : 8 * step + 8, :] = told
 
 
-def couple(nodes, per, steps, got, base, left, right, send, chain):
+def couple(nodes, per, steps, got, base, left, right, tree, send, chain):
     cols = left.shape[1]
     rank = lax.axis_index("gy")
-
-    def told(block, i):
-        return got[8 * block + i : 8 * block + i + 1, :]
-
-    zero = jnp.zeros((1, cols), F32)
-    g, offset, rho = zero, (zero, zero), zero
-    for block in range(steps):
-        a, b, c = told(block, 4), told(block, 5), told(block, 6)
-        first = [told(block, 0), told(block, 1)]
-        last = [told(block, 2), told(block, 3)]
-        pushed = [g * offset[0], g * offset[1]]
-        kappa = zero if block == 0 else g * (g * rho - 1.0) + STANDIN
-        inv = 1.0 / (1.0 - a * kappa)
-        start = [(first[i] + a * pushed[i]) * inv for i in range(2)]
-        slope = b * inv
-        for i, value in enumerate([start[0], start[1], slope, pushed[0], pushed[1], kappa]):
-            chain[block, i : i + 1, :] = value
-        offset = [last[i] + b * (pushed[i] + kappa * start[i]) for i in range(2)]
-        rho = c + b * kappa * slope
-        g = told(block, 7)
-    value = (zero, zero)
-    for block in reversed(range(steps)):
-        g = zero if block == steps - 1 else told(block, 7)
-        chain[block, 6:7, :] = value[0]
-        chain[block, 7:8, :] = value[1]
-        value = [chain[block, i : i + 1, :] + chain[block, 2:3, :] * (g * value[i]) for i in range(2)]
-    mine = chain[rank]
-    own = got[pl.ds(pl.multiple_of(8 * rank, 8), 8), :]
-    g_above = jnp.where(rank == steps - 1, 0.0, own[7:8])
-    for part in range(2):
-        upper = g_above * mine[6 + part : 7 + part]
-        here = mine[part : part + 1] + mine[2:3] * upper
-        lower = mine[3 + part : 4 + part] + mine[5:6] * here
-        for t in range(per):
-            rows = pl.ds(t * nodes, nodes)
+    first, last, a, b, c, gap = (
+        [got[pl.ds(i, steps, stride=8), :] for i in some] for some in ((0, 1), (2, 3), (4,), (5,), (6,), (7,))
+    )
+    a, b, c, gap = a[0], b[0], c[0], gap[0]
+    block = lax.broadcasted_iota(jnp.int32, (steps, cols), 0)
+    change = jnp.where(block == 0, 0.0, pltpu.roll(gap, 1, 0) - STANDIN)
+    scale = 1.0 / (1.0 + a * change)
+    first = [x * scale for x in first]
+    last = [last[n] - b * change * first[n] for n in range(2)]
+    a, b, c = a * scale, b * scale, c - b * b * change * scale
+    joins = joined(first, last, a, b, c, gap)[1]
+    for part in range(2):
+        lower, upper = parted(joins, part, jnp.zeros_like(a), jnp.zeros_like(a))
+        here = first[part] + a * lower + b * upper
+        chain[3 * part] = lower - change * here
+        chain[3 * part + 1] = upper
+        chain[3 * part + 2] = pltpu.roll(here, steps - 1, 0)
+    inner = [[tree[level, i] for i in range(8)] for level in range(LEVELS)]
+    length = left.shape[0] // SEGMENTS
+    for part in range(2):
+        lower, upper, after = (chain[3 * part + i, pl.ds(rank, 1), :] for i in range(3))
+        lower, upper = parted(inner, part, *(jnp.broadcast_to(x, (SEGMENTS, cols)) for x in (lower, upper)))
+        for t in range(length):
+            rows = pl.ds(t * SEGMENTS, SEGMENTS)
             solved = base[part, rows, :] + left[rows, :] * lower + right[rows, :] * upper
-            send[pl.ds(part * per + t, nodes, stride=SEND_C), :] = solved
-        send[pl.ds(2 * per + part, nodes, stride=SEND_C), :] = jnp.broadcast_to(
-            mine[6 + part : 7 + part], (nodes, cols)
-        )
-
-
-def inverse(nodes, per, got, across, along, turn, send, edge, pick):
+            spot = t // per * SEND_C + part * per + t % per
+            send[pl.ds(spot, SEGMENTS, stride=length // per * SEND_C), :] = solved
+        send[pl.ds(2 * per + part, nodes, stride=SEND_C), :] = jnp.broadcast_to(after, (nodes, cols))
+
+
+def inverse(nodes, per, got, across, across_full, along, along_full, turn, send, edge, pick):
     cols = got.shape[1]
     place = place_of(nodes)
 
@@ -319,10 +349,10 @@
         flow.append(jnp.concatenate([-kx * imag, kx * real], 1))
         plain.append(jnp.concatenate([real, imag], 1))
     plain.append(jnp.concatenate([slot(2 * per), slot(2 * per + 1)], 1))
-    plain = dot(jnp.concatenate(plain, 0), along[...])
-    flow = dot(jnp.concatenate(flow, 0), along[...], HIGH)
-    plain = dot(across[...], turned(plain))
-    flow = dot(across[...], turned(flow), HIGH)
+    plain = right_dot(jnp.concatenate(plain, 0), along_full[...], 3)
+    flow = right_dot(jnp.concatenate(flow, 0), along[...], 2)
+    plain = left_dot(across_full[...], turned(plain), 3)
+    flow = left_dot(across[...], turned(flow), 2)
     for i, done in enumerate((flow, plain)):
         for part in range(2):
             for t in range(per):
@@ -347,12 +377,12 @@
 
     for part in range(2):
         for t in range(per):
-            place = pl.ds(t * nodes, nodes)
+            place = pl.ds(t, nodes, stride=per)
             u_new[part, place, :] = u[part, place, :] - slot(part * per + t)
         copies[part].start()
     for part in range(2):
         for t in range(per):
-            pot[part, pl.ds(t * nodes, nodes), :] = slot((2 + part) * per + t)
+            pot[part, pl.ds(t, nodes, stride=per), :] = slot((2 + part) * per + t)
     for part in range(2):
         turned = KZ * pot[1 - part]
         w_new[part] = w[part] + (turned if part == 0 else -turned)
@@ -395,7 +425,7 @@
     shape = u_star.shape
     rows, cols = shape[2:]
     per, wider = rows // nodes, rows // GROUP
-    across_f, across_i, along_f, along_i, turn = tables(nodes, cols)
+    across_f, across_i, across_full, along_f, along_i, along_full, turn = tables(nodes, cols)
     u, v, w = (x.reshape(2, rows, cols) for x in (u_star, v_star, w_star))
     field, plane, line = (2, rows, cols), (rows, cols), (1, rows)
     ranks = order(nodes)
@@ -413,20 +443,20 @@
         got, across_f, along_f, turn
     )
     got = exchange(send, "gx", nodes, all_x)
-    base, left, right, send = call(
+    base, left, right, tree, send = call(
         functools.partial(eliminate, nodes),
-        [field, plane, plane, (8 * steps, cols)],
-        [field, plane],
+        [field, plane, plane, (LEVELS, 8, SEGMENTS, cols), (8 * steps, cols)],
+        [field],
         [VMEM] * 3,
     )(got, wide, heavy)
     got = exchange(send, "gy", steps)
     (send,) = call(
-        functools.partial(couple, nodes, per, steps), [(nodes * SEND_C, cols)], [(steps, 8, cols)], [VMEM] * 4
-    )(got, base, left, right)
+        functools.partial(couple, nodes, per, steps), [(nodes * SEND_C, cols)], [(6, steps, cols)], [VMEM] * 5
+    )(got, base, left, right, tree)
     got = exchange(send, "gx", nodes, all_x)
     send, edge = call(
-        functools.partial(inverse, nodes, per), [(nodes * SEND_D, cols), (8, cols)], [(2 * nodes, cols)], [VMEM] * 4
-    )(got, across_i, along_i, turn)
+        functools.partial(inverse, nodes, per), [(nodes * SEND_D, cols), (8, cols)], [(2 * nodes, cols)], [VMEM] * 6
+    )(got, across_i, across_full, along_i, along_full, turn)
     got = exchange(send, "gx", nodes, all_x)
     outs = call(
         functools.partial(finish, nodes, per, steps),

time: 85.2 us -> 84.7 us (level)
  no operation moved by 1% of the time
where the time goes in v5:
time: 84.7 us; the launch traced here: 84.3 us
  blocking collectives  80.2 us (95%)
  Pallas kernels  3.35 us (4%)
    all_to_all x5, blocking collectives, exchange(): lax.all_to_all(array, axis, 0, 0, axis_index_groups=groups, tiled=True)  80.2 us

profile of v5, /device:TPU:8, one launch (start us, length us, event | category | flops | bytes accessed | tf_op | source)
XLA Modules:
  0.0 84.3 jit_solution(6879506916107156119)
XLA Ops:
  0.6 0.0 copy-start.1
  0.6 1.1 %shard_map.139 = (f32[416,128]{1,0:T(8,128)S(1)}, f32[96,128]{1,0:T(8,128)S(1)}, f32[96,128]{1,0:T(8,128)S(1)}) custom-call(f32[2,96,128]{2,1,0:T(8,128)} %bitcast.30, f32[2,96,128]{2,1,0:T(8,128)} %bitcast.32, f32[2,96,128]{2,1,0:T(8,128)} %bitcast.34, f32[1,96]{1,0:T(1,128)} %bitcast.40, f32[1,96]{1,0:T(1,128)} %bitcast.41), custom_call_target="tpu_custom_call" | custom-call | flops 1000000 | bytes 1000000 | tf_op jit(solution)/shard_map/pallas_call | solution.py:434
  1.8 0.0 copy-start.6
  1.8 0.0 copy-start.8
  1.8 15.7 %all_to_all.45 = f32[16,1,3328]{2,1,0:T(1,128)S(1)} all-to-all(f32[16,1,3328]{2,1,0:T(1,128)S(1)} %bitcast.37), channel_id=1, replica_groups={{0,128,256,384,16,144,272,400,32,160,288,416,48,176,304,432},{64,192,32..., dimensions={0} | all-to-all | bytes 425984 | tf_op jit(solution)/shard_map/all_to_all | solution.py:420
  17.5 0.0 copy-done.1
  17.5 0.0 copy-done.6
  17.5 0.0 copy-done.8
  17.5 0.5 shard_map.140
  18.0 0.0 copy-start
  18.0 17.3 %all_to_all.46 = f32[32,1,1792]{2,1,0:T(1,128)S(1)} all-to-all(f32[32,1,1792]{2,1,0:T(1,128)S(1)} %bitcast.24), channel_id=1, replica_groups={{0,128,256,384,16,144,272,400,32,160,288,416,48,176,304,432,64,192,320,..., dimensions={0} | all-to-all | bytes 458752 | tf_op jit(solution)/shard_map/all_to_all | solution.py:420
  35.3 0.1 shard_map.141
  35.5 18.1 %all_to_all.47 = f32[16,1,1024]{2,1,0:T(1,128)S(1)} all-to-all(f32[16,1,1024]{2,1,0:T(1,128)S(1)} %bitcast.39), channel_id=1, replica_groups=mesh['gx'=32,'gy'=16] {'gy'}, dimensions={0} | all-to-all | bytes 131072 | tf_op jit(solution)/shard_map/all_to_all | solution.py:420
  53.6 0.0 copy-start.2
  53.6 0.2 shard_map.142
  53.8 0.0 copy-start.7
  53.8 0.0 copy-start.9
  53.8 14.6 %all_to_all.48 = f32[32,1,1024]{2,1,0:T(1,128)S(1)} all-to-all(f32[32,1,1024]{2,1,0:T(1,128)S(1)} %bitcast.28), channel_id=1, replica_groups={{0,128,256,384,16,144,272,400,32,160,288,416,48,176,304,432,64,192,320,..., dimensions={0} | all-to-all | bytes 262144 | tf_op jit(solution)/shard_map/all_to_all | solution.py:420
  68.4 0.0 copy-done
  68.4 0.0 copy-done.2
  68.4 0.0 copy-done.7
  68.4 0.0 copy-done.9
  68.4 0.6 shard_map.143
  69.0 0.0 copy-start.3
  69.0 0.0 copy-start.4
  69.0 0.0 copy-start.5
  69.1 14.5 %all_to_all.49 = f32[32,1,1536]{2,1,0:T(1,128)S(1)} all-to-all(f32[32,1,1536]{2,1,0:T(1,128)S(1)} %bitcast.38), channel_id=1, replica_groups={{0,128,256,384,16,144,272,400,32,160,288,416,48,176,304,432,64,192,320,..., dimensions={0} | all-to-all | bytes 393216 | tf_op jit(solution)/shard_map/all_to_all | solution.py:420
  83.6 0.0 copy-done.3
  83.6 0.0 copy-done.4
  83.6 0.0 copy-done.5
  83.6 0.8 shard_map.144
Async XLA Ops:
  0.6 16.9 %copy-start.1 = (bf16[768,256]{1,0:T(8,128)(2,1)S(1)}, bf16[768,256]{1,0:T(8,128)(2,1)}, u32[]{:S(2)}) copy-start(bf16[768,256]{1,0:T(8,128)(2,1)} %constant.15.clone.along) | copy-start | bytes 1179652
  1.8 15.7 %copy-start.6 = (f32[2,32,128]{2,1,0:T(8,128)S(1)}, f32[2,32,128]{2,1,0:T(8,128)}, u32[]{:S(2)}) copy-start(f32[2,32,128]{2,1,0:T(8,128)} %constant.16.clone.turn) | copy-start | bytes 98308
  1.8 15.7 %copy-start.8 = (bf16[2,64,96]{2,1,0:T(8,128)(2,1)S(1)}, bf16[2,64,96]{2,1,0:T(8,128)(2,1)}, u32[]{:S(2)}) copy-start(bf16[2,64,96]{2,1,0:T(8,128)(2,1)} %constant.14.clone.across) | copy-start | bytes 73732
  18.0 50.4 %copy-start = (bf16[1536,256]{1,0:T(8,128)(2,1)S(1)}, bf16[1536,256]{1,0:T(8,128)(2,1)}, u32[]{:S(2)}) copy-start(bf16[1536,256]{1,0:T(8,128)(2,1)} %constant.20.clone.along_full) | copy-start | bytes 2359300
  53.6 14.8 %copy-start.2 = (bf16[768,256]{1,0:T(8,128)(2,1)S(1)}, bf16[768,256]{1,0:T(8,128)(2,1)}, u32[]{:S(2)}) copy-start(bf16[768,256]{1,0:T(8,128)(2,1)} %constant.19.clone.along) | copy-start | bytes 1179652
  53.8 14.6 %copy-start.7 = (bf16[64,384]{1,0:T(8,128)(2,1)S(1)}, bf16[64,384]{1,0:T(8,128)(2,1)}, u32[]{:S(2)}) copy-start(bf16[64,384]{1,0:T(8,128)(2,1)} %constant.18.clone.across_full) | copy-start | bytes 147460
  53.8 14.6 %copy-start.9 = (bf16[64,192]{1,0:T(8,128)(2,1)S(1)}, bf16[64,192]{1,0:T(8,128)(2,1)}, u32[]{:S(2)}) copy-start(bf16[64,192]{1,0:T(8,128)(2,1)} %constant.17.clone.across) | copy-start | bytes 73732
  69.0 14.5 %copy-start.3 = (f32[2,1,96,128]{3,2,1,0:T(8,128)S(1)}, f32[2,1,96,128]{3,2,1,0:T(8,128)}, u32[]{:S(2)}) copy-start(f32[2,1,96,128]{3,2,1,0:T(8,128)} %param.12) | copy-start | bytes 294916
  69.0 14.5 %copy-start.4 = (f32[2,1,96,128]{3,2,1,0:T(8,128)S(1)}, f32[2,1,96,128]{3,2,1,0:T(8,128)}, u32[]{:S(2)}) copy-start(f32[2,1,96,128]{3,2,1,0:T(8,128)} %param.13) | copy-start | bytes 294916
  69.0 14.5 %copy-start.5 = (f32[2,1,96,128]{3,2,1,0:T(8,128)S(1)}, f32[2,1,96,128]{3,2,1,0:T(8,128)}, u32[]{:S(2)}) copy-start(f32[2,1,96,128]{3,2,1,0:T(8,128)} %param.14) | copy-start | bytes 294916

commit v6 on v5

--- a/solution.py
+++ b/solution.py
@@ -20,20 +20,19 @@
 GROUP = ALONG * BESIDE
 LEVELS = 3
 SEGMENTS = 2**LEVELS
-SEND_C, SEND_D = 8, 12
+
+
+PLACES = [(2, 2), (1, 1), (3, 0), (2, 1), (3, 2), (0, 3), (0, 0), (2, 0), (3, 1), (0, 2), (3, 3), (1, 2), (2, 3), (0, 1), (1, 0), (1, 3)]
 
 
 def order(nodes):
     breadth = nodes // ALONG
-    return [
-        breadth * x + BESIDE * q + y for q in range(breadth // BESIDE) for y in range(BESIDE) for x in range(ALONG)
-    ]
+    return [breadth * x + BESIDE * q + y for q in range(breadth // BESIDE) for x, y in PLACES]
 
 
 def place_of(nodes):
     rank = lax.axis_index("gx")
-    x, y = rank // (nodes // ALONG), rank % (nodes // ALONG)
-    return y // BESIDE * GROUP + y % BESIDE * ALONG + x
+    return sum(jnp.where(rank == other, place, 0) for place, other in enumerate(order(nodes)))
 
 
 def tables(nodes, cols):
@@ -52,7 +51,12 @@
         ]
     )
     c, s = cos_sin(ranks, residues, nodes)
-    across_i = np.block([[c, -s], [s, c]])
+    across_i = np.stack(
+        [
+            np.block([[c[i : i + GROUP], -s[i : i + GROUP]], [s[i : i + GROUP], c[i : i + GROUP]]])
+            for i in range(0, nodes, GROUP)
+        ]
+    )
     c, s = cos_sin(places, places, cols)
     along_f = np.block([[c, -s], [s, c]])
     along_i = np.block([[c, s], [-s, c]]) / full
@@ -135,9 +139,16 @@
     wide[...] = h
     copies[1].wait()
     heavy[...] = column(weight[...], rows, cols)
+    to_each = 4 * per + 2
+
+    def pack(field):
+        for t in range(per):
+            send[pl.ds(field * per + t, GROUP, stride=to_each), :] = tmp[field, pl.ds(t * GROUP, GROUP), :]
+
     copies[2].wait()
     for part in range(2):
         tmp[part] = -h * u[part]
+        pack(part)
     copies[3].wait()
     copies[4].wait()
     first = lax.broadcasted_iota(jnp.int32, (rows, cols), 0) == 0
@@ -146,11 +157,7 @@
         below = jnp.where(first, 0.0, pltpu.roll(now, 1, 0))
         other = w[1 - part] * (h * KZ)
         tmp[2 + part] = below - now + (other if part == 0 else -other)
-    to_each = 4 * per + 2
-    for field in range(4):
-        for t in range(per):
-            send[pl.ds(field * per + t, GROUP, stride=to_each), :] = tmp[field, pl.ds(t * GROUP, GROUP), :]
-    for part in range(2):
+        pack(2 + part)
         last = jnp.broadcast_to(v[part, rows - 1 : rows, :], (GROUP, cols))
         send[pl.ds(4 * per + part, GROUP, stride=to_each), :] = last
 
@@ -158,7 +165,7 @@
 def forward(nodes, got, across, along, turn, send):
     cols = got.shape[1]
     per = (got.shape[0] // GROUP - 2) // 4
-    group = place_of(nodes) // GROUP
+    group, place = place_of(nodes) // GROUP, place_of(nodes) % GROUP
 
     def slot(s):
         return got[pl.ds(s, GROUP, stride=4 * per + 2), :]
@@ -175,15 +182,14 @@
         turned.append(jnp.concatenate([a * c + b * s, b * c - a * s], 1))
     spectrum = right_dot(jnp.concatenate(turned, 0), along[...], 2)
     kx = wavenumbers(nodes, cols)
-    to_each = 2 * per + 2
+    to_each = 2 * per + 1
     for t in range(per):
         u = spectrum[t * nodes : (t + 1) * nodes]
         g = spectrum[(per + t) * nodes : (per + t + 1) * nodes]
         send[pl.ds(t, nodes, stride=to_each), :] = g[:, :cols] - kx * u[:, cols:]
         send[pl.ds(per + t, nodes, stride=to_each), :] = g[:, cols:] + kx * u[:, :cols]
     last = spectrum[2 * per * nodes :]
-    for part in range(2):
-        send[pl.ds(2 * per + part, nodes, stride=to_each), :] = last[:, part * cols : (part + 1) * cols]
+    send[pl.ds(2 * per, nodes, stride=to_each), :] = jnp.where(place % 2 == 0, last[:, :cols], last[:, cols:])
 
 
 def joined(first, last, a, b, c, gap):
@@ -227,7 +233,7 @@
     steps = lax.axis_size("gy")
     rank_x, rank_y = place_of(nodes), lax.axis_index("gy")
     per = rows // GROUP
-    to_each = 2 * per + 2
+    to_each = 2 * per + 1
 
     def summed(s, count):
         return sum(got[pl.ds(to_each * i + s, count, stride=to_each), :] for i in range(0, nodes, GROUP))
@@ -235,7 +241,7 @@
     for part in range(2):
         for t in range(per):
             rhs[part, pl.ds(t * GROUP, GROUP), :] = summed(part * per + t, GROUP)
-    edge = [summed(2 * per + part, 1) for part in range(2)]
+    edge = [summed(2 * per + part * to_each, 1) for part in range(2)]
     place = lax.broadcasted_iota(jnp.int32, (SEGMENTS, cols), 1)
     run = lax.broadcasted_iota(jnp.int32, (SEGMENTS, cols), 0)
     kx = signed_half(rank_x + nodes * place, nodes * cols)
@@ -292,7 +298,7 @@
         send[8 * step : 8 * step + 8, :] = told
 
 
-def couple(nodes, per, steps, got, base, left, right, tree, send, chain):
+def couple(nodes, steps, got, base, left, right, tree, send, chain):
     cols = left.shape[1]
     rank = lax.axis_index("gy")
     first, last, a, b, c, gap = (
@@ -314,23 +320,27 @@
         chain[3 * part + 2] = pltpu.roll(here, steps - 1, 0)
     inner = [[tree[level, i] for i in range(8)] for level in range(LEVELS)]
     length = left.shape[0] // SEGMENTS
+    per = left.shape[0] // GROUP
+    to_each = 2 * per + 2
     for part in range(2):
         lower, upper, after = (chain[3 * part + i, pl.ds(rank, 1), :] for i in range(3))
         lower, upper = parted(inner, part, *(jnp.broadcast_to(x, (SEGMENTS, cols)) for x in (lower, upper)))
         for t in range(length):
             rows = pl.ds(t * SEGMENTS, SEGMENTS)
             solved = base[part, rows, :] + left[rows, :] * lower + right[rows, :] * upper
-            spot = t // per * SEND_C + part * per + t % per
-            send[pl.ds(spot, SEGMENTS, stride=length // per * SEND_C), :] = solved
-        send[pl.ds(2 * per + part, nodes, stride=SEND_C), :] = jnp.broadcast_to(after, (nodes, cols))
-
-
-def inverse(nodes, per, got, across, across_full, along, along_full, turn, send, edge, pick):
+            spot = t // per * to_each + part * per + t % per
+            for group in range(0, nodes, GROUP):
+                send[pl.ds(group * to_each + spot, SEGMENTS, stride=length // per * to_each), :] = solved
+        send[pl.ds(2 * per + part, nodes, stride=to_each), :] = jnp.broadcast_to(after, (nodes, cols))
+
+
+def inverse(nodes, got, across, across_full, along, along_full, turn, send, edge, pick):
     cols = got.shape[1]
-    place = place_of(nodes)
+    per = got.shape[0] // nodes // 2 - 1
+    group, place = place_of(nodes) // GROUP, place_of(nodes) % GROUP
 
     def slot(s):
-        return got[pl.ds(s, nodes, stride=SEND_C), :]
+        return got[pl.ds(s, nodes, stride=2 * per + 2), :]
 
     def turned(begun):
         c, s = turn[0], turn[1]
@@ -351,20 +361,21 @@
     plain.append(jnp.concatenate([slot(2 * per), slot(2 * per + 1)], 1))
     plain = right_dot(jnp.concatenate(plain, 0), along_full[...], 3)
     flow = right_dot(jnp.concatenate(flow, 0), along[...], 2)
-    plain = left_dot(across_full[...], turned(plain), 3)
-    flow = left_dot(across[...], turned(flow), 2)
+    plain = left_dot(across_full[group], turned(plain), 3)
+    flow = left_dot(across[group], turned(flow), 2)
     for i, done in enumerate((flow, plain)):
         for part in range(2):
             for t in range(per):
-                block = done[part * nodes : (part + 1) * nodes, t * cols : (t + 1) * cols]
-                send[pl.ds((2 * i + part) * per + t, nodes, stride=SEND_D), :] = block
+                block = done[part * GROUP : (part + 1) * GROUP, t * cols : (t + 1) * cols]
+                send[pl.ds((2 * i + part) * per + t, GROUP, stride=4 * per), :] = block
     pick[...] = plain[:, per * cols :]
     for part in range(2):
-        edge[part : part + 1, :] = pick[pl.ds(place + part * nodes, 1), :]
-
-
-def finish(nodes, per, steps, u, v, w, got, edge, heavy, u_far, v_far, w_far, u_new, v_new, w_new, pot, left):
+        edge[part : part + 1, :] = pick[pl.ds(place + part * GROUP, 1), :]
+
+
+def finish(steps, u, v, w, got, edge, heavy, u_far, v_far, w_far, u_new, v_new, w_new, pot, left):
     rows, cols = heavy.shape
+    per = rows // GROUP
     rank = lax.axis_index("gy")
     copies = [
         pltpu.make_async_copy(near.at[part], far.at[part], left.at[2 * i + part])
@@ -373,16 +384,16 @@
     ]
 
     def slot(s):
-        return got[pl.ds(s, nodes, stride=SEND_D), :]
+        return got[pl.ds(s, GROUP, stride=4 * per), :]
 
     for part in range(2):
         for t in range(per):
-            place = pl.ds(t, nodes, stride=per)
+            place = pl.ds(t, GROUP, stride=per)
             u_new[part, place, :] = u[part, place, :] - slot(part * per + t)
         copies[part].start()
     for part in range(2):
         for t in range(per):
-            pot[part, pl.ds(t, nodes, stride=per), :] = slot((2 + part) * per + t)
+            pot[part, pl.ds(t, GROUP, stride=per), :] = slot((2 + part) * per + t)
     for part in range(2):
         turned = KZ * pot[1 - part]
         w_new[part] = w[part] + (turned if part == 0 else -turned)
@@ -424,7 +435,7 @@
     nodes, steps = lax.axis_size("gx"), lax.axis_size("gy")
     shape = u_star.shape
     rows, cols = shape[2:]
-    per, wider = rows // nodes, rows // GROUP
+    wider = rows // GROUP
     across_f, across_i, across_full, along_f, along_i, along_full, turn = tables(nodes, cols)
     u, v, w = (x.reshape(2, rows, cols) for x in (u_star, v_star, w_star))
     field, plane, line = (2, rows, cols), (rows, cols), (1, rows)
@@ -439,7 +450,7 @@
         semaphores=5,
     )(*(pltpu.with_memory_space_constraint(x, pltpu.HBM) for x in (u, v, w, cell_width.reshape(line), face_weight.reshape(line))))
     got = exchange(send, "gx", GROUP, near)
-    (send,) = call(functools.partial(forward, nodes), [(nodes * (2 * wider + 2), cols)], [], [VMEM] * 4)(
+    (send,) = call(functools.partial(forward, nodes), [(nodes * (2 * wider + 1), cols)], [], [VMEM] * 4)(
         got, across_f, along_f, turn
     )
     got = exchange(send, "gx", nodes, all_x)
@@ -451,15 +462,15 @@
     )(got, wide, heavy)
     got = exchange(send, "gy", steps)
     (send,) = call(
-        functools.partial(couple, nodes, per, steps), [(nodes * SEND_C, cols)], [(6, steps, cols)], [VMEM] * 5
+        functools.partial(couple, nodes, steps), [(nodes * (2 * wider + 2), cols)], [(6, steps, cols)], [VMEM] * 5
     )(got, base, left, right, tree)
     got = exchange(send, "gx", nodes, all_x)
     send, edge = call(
-        functools.partial(inverse, nodes, per), [(nodes * SEND_D, cols), (8, cols)], [(2 * nodes, cols)], [VMEM] * 6
+        functools.partial(inverse, nodes), [(GROUP * 4 * wider, cols), (8, cols)], [(2 * GROUP, cols)], [VMEM] * 6
     )(got, across_i, across_full, along_i, along_full, turn)
-    got = exchange(send, "gx", nodes, all_x)
+    got = exchange(send, "gx", GROUP, near)
     outs = call(
-        functools.partial(finish, nodes, per, steps),
+        functools.partial(finish, steps),
         [field] * 3,
         [field] * 4,
         [VMEM] * 6,

time: 84.7 us -> 82 us (0.968)
  the two profiles are of different devices: /device:TPU:8 before, /device:TPU:4 now
where the time goes in v6:
time: 82 us; the launch traced here: 81.6 us
  blocking collectives  77.2 us (94%)
  Pallas kernels  3.58 us (4%)
    all_to_all x5, blocking collectives, exchange(): lax.all_to_all(array, axis, 0, 0, axis_index_groups=groups, tiled=True)  77.2 us

profile of v6, /device:TPU:4, one launch (start us, length us, event | category | flops | bytes accessed | tf_op | source)
XLA Modules:
  0.0 81.6 jit_solution(16710791731759032568)
XLA Ops:
  0.6 0.0 copy-start.1
  0.6 1.1 %shard_map.139 = (f32[416,128]{1,0:T(8,128)S(1)}, f32[96,128]{1,0:T(8,128)S(1)}, f32[96,128]{1,0:T(8,128)S(1)}) custom-call(f32[2,96,128]{2,1,0:T(8,128)} %bitcast.30, f32[2,96,128]{2,1,0:T(8,128)} %bitcast.32, f32[2,96,128]{2,1,0:T(8,128)} %bitcast.34, f32[1,96]{1,0:T(1,128)} %bitcast.40, f32[1,96]{1,0:T(1,128)} %bitcast.41), custom_call_target="tpu_custom_call" | custom-call | flops 1000000 | bytes 1000000 | tf_op jit(solution)/shard_map/pallas_call | solution.py:445
  1.8 0.0 copy-start.6
  1.8 0.0 copy-start.8
  1.8 16.6 %all_to_all.45 = f32[16,1,3328]{2,1,0:T(1,128)S(1)} all-to-all(f32[16,1,3328]{2,1,0:T(1,128)S(1)} %bitcast.37), channel_id=1, replica_groups={{288,144,384,272,416,48,0,256,400,32,432,160,304,16,128,176},{352,208,4..., dimensions={0} | all-to-all | bytes 425984 | tf_op jit(solution)/shard_map/all_to_all | solution.py:431
  18.5 0.0 copy-done.1
  18.5 0.0 copy-done.6
  18.5 0.0 copy-done.8
  18.5 0.5 shard_map.140
  19.0 13.8 %all_to_all.46 = f32[32,1,1664]{2,1,0:T(1,128)S(1)} all-to-all(f32[32,1,1664]{2,1,0:T(1,128)S(1)} %bitcast.27), channel_id=1, replica_groups={{288,144,384,272,416,48,0,256,400,32,432,160,304,16,128,176,352,208,448..., dimensions={0} | all-to-all | bytes 425984 | tf_op jit(solution)/shard_map/all_to_all | solution.py:431
  32.7 0.0 copy-start
  32.7 0.2 shard_map.141
  32.9 18.3 %all_to_all.47 = f32[16,1,1024]{2,1,0:T(1,128)S(1)} all-to-all(f32[16,1,1024]{2,1,0:T(1,128)S(1)} %bitcast.39), channel_id=1, replica_groups=mesh['gx'=32,'gy'=16] {'gy'}, dimensions={0} | all-to-all | bytes 131072 | tf_op jit(solution)/shard_map/all_to_all | solution.py:431
  51.2 0.0 copy-start.2
  51.2 0.1 shard_map.142
  51.4 0.0 copy-start.7
  51.4 0.0 copy-start.9
  51.4 16.1 %all_to_all.48 = f32[32,1,1792]{2,1,0:T(1,128)S(1)} all-to-all(f32[32,1,1792]{2,1,0:T(1,128)S(1)} %bitcast.24), channel_id=1, replica_groups={{288,144,384,272,416,48,0,256,400,32,432,160,304,16,128,176,352,208,448..., dimensions={0} | all-to-all | bytes 458752 | tf_op jit(solution)/shard_map/all_to_all | solution.py:431
  67.5 0.0 copy-done
  67.5 0.0 copy-done.2
  67.5 0.0 copy-done.7
  67.5 0.0 copy-done.9
  67.5 0.8 %shard_map.143 = (f32[384,128]{1,0:T(8,128)S(1)}, f32[8,128]{1,0:T(8,128)S(1)}) custom-call(f32[448,128]{1,0:T(8,128)S(1)} %bitcast.25, bf16[2,32,192]{2,1,0:T(8,128)(2,1)S(1)} %copy-done.9, bf16[2,32,384]{2,1,0:T(8,128)(2,1)S(1)} %copy-done.7, bf16[768,256]{1,0:T(8,128)(2,1)S(1)} %copy-done.2, bf16[1536,256]{1,0:T(8,128)(2,1)S(1)} %copy-done, ...), custom_call_target="tpu_custom_call" | custom-call | flops 1000000 | bytes 1000000 | tf_op jit(solution)/shard_map/pallas_call | solution.py:468
  68.4 0.0 copy-start.3
  68.4 0.0 copy-start.4
  68.4 0.0 copy-start.5
  68.4 12.4 %all_to_all.49 = f32[16,1,3072]{2,1,0:T(1,128)S(1)} all-to-all(f32[16,1,3072]{2,1,0:T(1,128)S(1)} %bitcast.38), channel_id=1, replica_groups={{288,144,384,272,416,48,0,256,400,32,432,160,304,16,128,176},{352,208,4..., dimensions={0} | all-to-all | bytes 393216 | tf_op jit(solution)/shard_map/all_to_all | solution.py:431
  80.9 0.0 copy-done.3
  80.9 0.0 copy-done.4
  80.9 0.0 copy-done.5
  80.9 0.8 shard_map.144
Async XLA Ops:
  0.6 17.8 %copy-start.1 = (bf16[768,256]{1,0:T(8,128)(2,1)S(1)}, bf16[768,256]{1,0:T(8,128)(2,1)}, u32[]{:S(2)}) copy-start(bf16[768,256]{1,0:T(8,128)(2,1)} %constant.15.clone.along) | copy-start | bytes 1179652
  1.8 16.7 %copy-start.6 = (f32[2,32,128]{2,1,0:T(8,128)S(1)}, f32[2,32,128]{2,1,0:T(8,128)}, u32[]{:S(2)}) copy-start(f32[2,32,128]{2,1,0:T(8,128)} %constant.16.clone.turn) | copy-start | bytes 98308
  1.8 16.7 %copy-start.8 = (bf16[2,64,96]{2,1,0:T(8,128)(2,1)S(1)}, bf16[2,64,96]{2,1,0:T(8,128)(2,1)}, u32[]{:S(2)}) copy-start(bf16[2,64,96]{2,1,0:T(8,128)(2,1)} %constant.14.clone.across) | copy-start | bytes 73732
  32.7 34.8 %copy-start = (bf16[1536,256]{1,0:T(8,128)(2,1)S(1)}, bf16[1536,256]{1,0:T(8,128)(2,1)}, u32[]{:S(2)}) copy-start(bf16[1536,256]{1,0:T(8,128)(2,1)} %constant.20.clone.along_full) | copy-start | bytes 2359300
  51.2 16.3 %copy-start.2 = (bf16[768,256]{1,0:T(8,128)(2,1)S(1)}, bf16[768,256]{1,0:T(8,128)(2,1)}, u32[]{:S(2)}) copy-start(bf16[768,256]{1,0:T(8,128)(2,1)} %constant.19.clone.along) | copy-start | bytes 1179652
  51.4 16.2 %copy-start.7 = (bf16[2,32,384]{2,1,0:T(8,128)(2,1)S(1)}, bf16[2,32,384]{2,1,0:T(8,128)(2,1)}, u32[]{:S(2)}) copy-start(bf16[2,32,384]{2,1,0:T(8,128)(2,1)} %constant.18.clone.across_full) | copy-start | bytes 147460
  51.4 16.2 %copy-start.9 = (bf16[2,32,192]{2,1,0:T(8,128)(2,1)S(1)}, bf16[2,32,192]{2,1,0:T(8,128)(2,1)}, u32[]{:S(2)}) copy-start(bf16[2,32,192]{2,1,0:T(8,128)(2,1)} %constant.17.clone.across) | copy-start | bytes 73732
  68.4 12.5 %copy-start.3 = (f32[2,1,96,128]{3,2,1,0:T(8,128)S(1)}, f32[2,1,96,128]{3,2,1,0:T(8,128)}, u32[]{:S(2)}) copy-start(f32[2,1,96,128]{3,2,1,0:T(8,128)} %param.12) | copy-start | bytes 294916
  68.4 12.5 %copy-start.4 = (f32[2,1,96,128]{3,2,1,0:T(8,128)S(1)}, f32[2,1,96,128]{3,2,1,0:T(8,128)}, u32[]{:S(2)}) copy-start(f32[2,1,96,128]{3,2,1,0:T(8,128)} %param.13) | copy-start | bytes 294916
  68.4 12.5 %copy-start.5 = (f32[2,1,96,128]{3,2,1,0:T(8,128)S(1)}, f32[2,1,96,128]{3,2,1,0:T(8,128)}, u32[]{:S(2)}) copy-start(f32[2,1,96,128]{3,2,1,0:T(8,128)} %param.14) | copy-start | bytes 294916

commit v7 on v6

--- a/solution.py
+++ b/solution.py
@@ -22,17 +22,18 @@
 SEGMENTS = 2**LEVELS
 
 
-PLACES = [(2, 2), (1, 1), (3, 0), (2, 1), (3, 2), (0, 3), (0, 0), (2, 0), (3, 1), (0, 2), (3, 3), (1, 2), (2, 3), (0, 1), (1, 0), (1, 3)]
-
-
-def order(nodes):
+OUT = [(2, 2), (1, 1), (0, 3), (1, 2), (2, 3), (3, 0), (0, 0), (0, 2), (1, 3), (2, 0), (3, 3), (2, 1), (3, 2), (1, 0), (0, 1), (3, 1)]
+BACK = [(2, 2), (1, 1), (3, 0), (2, 1), (3, 2), (0, 3), (0, 0), (2, 0), (3, 1), (0, 2), (3, 3), (1, 2), (2, 3), (0, 1), (1, 0), (1, 3)]
+
+
+def order(nodes, places):
     breadth = nodes // ALONG
-    return [breadth * x + BESIDE * q + y for q in range(breadth // BESIDE) for x, y in PLACES]
-
-
-def place_of(nodes):
+    return [breadth * x + BESIDE * q + y for q in range(breadth // BESIDE) for x, y in places]
+
+
+def place_of(nodes, places):
     rank = lax.axis_index("gx")
-    return sum(jnp.where(rank == other, place, 0) for place, other in enumerate(order(nodes)))
+    return sum(jnp.where(rank == other, place, 0) for place, other in enumerate(order(nodes, places)))
 
 
 def tables(nodes, cols):
@@ -42,7 +43,7 @@
         angle = 2.0 * np.pi * (np.outer(a, b) % length) / length
         return np.cos(angle), np.sin(angle)
 
-    ranks, residues, places = np.array(order(nodes)), np.arange(nodes), np.arange(cols)
+    ranks, residues, places = np.array(order(nodes, OUT)), np.arange(nodes), np.arange(cols)
     c, s = cos_sin(residues, ranks, nodes)
     across_f = np.stack(
         [
@@ -50,7 +51,9 @@
             for i in range(0, nodes, GROUP)
         ]
     )
-    c, s = cos_sin(ranks, residues, nodes)
+    ranks = order(nodes, BACK)
+    held = np.argsort(order(nodes, OUT))[ranks]
+    c, s = cos_sin(np.array(ranks), held, nodes)
     across_i = np.stack(
         [
             np.block([[c[i : i + GROUP], -s[i : i + GROUP]], [s[i : i + GROUP], c[i : i + GROUP]]])
@@ -60,7 +63,9 @@
     c, s = cos_sin(places, places, cols)
     along_f = np.block([[c, -s], [s, c]])
     along_i = np.block([[c, s], [-s, c]]) / full
-    turn = np.stack(cos_sin(residues, places, full))
+    turn_f, turn_i = np.stack(cos_sin(residues, places, full)), np.stack(cos_sin(held, places, full))
+    wave = held[:, None] + nodes * places
+    waves = np.where(wave < full // 2, wave, wave - full) * FLOW_FACTOR
     return [
         constant_side(across_f, -1, 2),
         constant_side(across_i, -1, 2),
@@ -68,7 +73,7 @@
         constant_side(along_f, 0, 2),
         constant_side(along_i, 0, 2),
         constant_side(along_i, 0, 3),
-        np.asarray(turn, np.float32),
+        *(np.asarray(x, np.float32) for x in (turn_f, turn_i, waves)),
     ]
 
 
@@ -165,7 +170,7 @@
 def forward(nodes, got, across, along, turn, send):
     cols = got.shape[1]
     per = (got.shape[0] // GROUP - 2) // 4
-    group, place = place_of(nodes) // GROUP, place_of(nodes) % GROUP
+    group, place = place_of(nodes, OUT) // GROUP, place_of(nodes, OUT) % GROUP
 
     def slot(s):
         return got[pl.ds(s, GROUP, stride=4 * per + 2), :]
@@ -231,7 +236,7 @@
     rows, cols = wide.shape
     length = rows // SEGMENTS
     steps = lax.axis_size("gy")
-    rank_x, rank_y = place_of(nodes), lax.axis_index("gy")
+    rank_x, rank_y = place_of(nodes, OUT), lax.axis_index("gy")
     per = rows // GROUP
     to_each = 2 * per + 1
 
@@ -334,10 +339,10 @@
         send[pl.ds(2 * per + part, nodes, stride=to_each), :] = jnp.broadcast_to(after, (nodes, cols))
 
 
-def inverse(nodes, got, across, across_full, along, along_full, turn, send, edge, pick):
+def inverse(nodes, got, across, across_full, along, along_full, turn, waves, send, edge, pick):
     cols = got.shape[1]
     per = got.shape[0] // nodes // 2 - 1
-    group, place = place_of(nodes) // GROUP, place_of(nodes) % GROUP
+    group, place = place_of(nodes, BACK) // GROUP, place_of(nodes, BACK) % GROUP
 
     def slot(s):
         return got[pl.ds(s, nodes, stride=2 * per + 2), :]
@@ -352,7 +357,7 @@
             imag.append(b * c + a * s)
         return jnp.concatenate([jnp.concatenate(real, 1), jnp.concatenate(imag, 1)], 0)
 
-    kx = wavenumbers(nodes, cols)
+    kx = waves[...]
     flow, plain = [], []
     for t in range(per):
         real, imag = slot(t), slot(per + t)
@@ -436,11 +441,13 @@
     shape = u_star.shape
     rows, cols = shape[2:]
     wider = rows // GROUP
-    across_f, across_i, across_full, along_f, along_i, along_full, turn = tables(nodes, cols)
+    across_f, across_i, across_full, along_f, along_i, along_full, turn_f, turn_i, waves = tables(nodes, cols)
     u, v, w = (x.reshape(2, rows, cols) for x in (u_star, v_star, w_star))
     field, plane, line = (2, rows, cols), (rows, cols), (1, rows)
-    ranks = order(nodes)
-    near, all_x = [ranks[i : i + GROUP] for i in range(0, nodes, GROUP)], [ranks]
+    (near_out, all_out), (near_back, all_back) = (
+        ([ranks[i : i + GROUP] for i in range(0, nodes, GROUP)], [ranks])
+        for ranks in (order(nodes, OUT), order(nodes, BACK))
+    )
 
     send, wide, heavy = call(
         prepare,
@@ -449,11 +456,11 @@
         [HBM] * 5,
         semaphores=5,
     )(*(pltpu.with_memory_space_constraint(x, pltpu.HBM) for x in (u, v, w, cell_width.reshape(line), face_weight.reshape(line))))
-    got = exchange(send, "gx", GROUP, near)
+    got = exchange(send, "gx", GROUP, near_out)
     (send,) = call(functools.partial(forward, nodes), [(nodes * (2 * wider + 1), cols)], [], [VMEM] * 4)(
-        got, across_f, along_f, turn
-    )
-    got = exchange(send, "gx", nodes, all_x)
+        got, across_f, along_f, turn_f
+    )
+    got = exchange(send, "gx", nodes, all_out)
     base, left, right, tree, send = call(
         functools.partial(eliminate, nodes),
         [field, plane, plane, (LEVELS, 8, SEGMENTS, cols), (8 * steps, cols)],
@@ -464,11 +471,11 @@
     (send,) = call(
         functools.partial(couple, nodes, steps), [(nodes * (2 * wider + 2), cols)], [(6, steps, cols)], [VMEM] * 5
     )(got, base, left, right, tree)
-    got = exchange(send, "gx", nodes, all_x)
+    got = exchange(send, "gx", nodes, all_back)
     send, edge = call(
-        functools.partial(inverse, nodes), [(GROUP * 4 * wider, cols), (8, cols)], [(2 * GROUP, cols)], [VMEM] * 6
-    )(got, across_i, across_full, along_i, along_full, turn)
-    got = exchange(send, "gx", GROUP, near)
+        functools.partial(inverse, nodes), [(GROUP * 4 * wider, cols), (8, cols)], [(2 * GROUP, cols)], [VMEM] * 7
+    )(got, across_i, across_full, along_i, along_full, turn_i, waves)
+    got = exchange(send, "gx", GROUP, near_back)
     outs = call(
         functools.partial(finish, steps),
         [field] * 3,

time: 82 us -> 81.8 us (level)
  no operation moved by 1% of the time
where the time goes in v7:
time: 81.8 us; the launch traced here: 81.4 us
  blocking collectives  77 us (94%)
  Pallas kernels  3.59 us (4%)
    all_to_all x5, blocking collectives, exchange(): lax.all_to_all(array, axis, 0, 0, axis_index_groups=groups, tiled=True)  77 us

profile of v7, /device:TPU:4, one launch (start us, length us, event | category | flops | bytes accessed | tf_op | source)
XLA Modules:
  0.0 81.4 jit_solution(13805894305414097228)
XLA Ops:
  0.6 0.0 copy-start.1
  0.6 1.1 %shard_map.157 = (f32[416,128]{1,0:T(8,128)S(1)}, f32[96,128]{1,0:T(8,128)S(1)}, f32[96,128]{1,0:T(8,128)S(1)}) custom-call(f32[2,96,128]{2,1,0:T(8,128)} %bitcast.30, f32[2,96,128]{2,1,0:T(8,128)} %bitcast.32, f32[2,96,128]{2,1,0:T(8,128)} %bitcast.34, f32[1,96]{1,0:T(1,128)} %bitcast.40, f32[1,96]{1,0:T(1,128)} %bitcast.41), custom_call_target="tpu_custom_call" | custom-call | flops 1000000 | bytes 1000000 | tf_op jit(solution)/shard_map/pallas_call | solution.py:452
  1.8 0.0 copy-start.7
  1.8 0.0 copy-start.8
  1.8 16.1 %all_to_all.45 = f32[16,1,3328]{2,1,0:T(1,128)S(1)} all-to-all(f32[16,1,3328]{2,1,0:T(1,128)S(1)} %bitcast.37), channel_id=1, replica_groups={{288,144,48,160,304,384,0,32,176,256,432,272,416,128,16,400},{352,208,1..., dimensions={0} | all-to-all | bytes 425984 | tf_op jit(solution)/shard_map/all_to_all | solution.py:436
  17.9 0.0 copy-done.1
  17.9 0.0 copy-done.7
  17.9 0.0 copy-done.8
  17.9 0.5 shard_map.158
  18.4 14.5 %all_to_all.46 = f32[32,1,1664]{2,1,0:T(1,128)S(1)} all-to-all(f32[32,1,1664]{2,1,0:T(1,128)S(1)} %bitcast.27), channel_id=1, replica_groups={{288,144,48,160,304,384,0,32,176,256,432,272,416,128,16,400,352,208,112..., dimensions={0} | all-to-all | bytes 425984 | tf_op jit(solution)/shard_map/all_to_all | solution.py:436
  32.9 0.0 copy-start
  32.9 0.2 shard_map.159
  33.1 18.2 %all_to_all.47 = f32[16,1,1024]{2,1,0:T(1,128)S(1)} all-to-all(f32[16,1,1024]{2,1,0:T(1,128)S(1)} %bitcast.39), channel_id=1, replica_groups=mesh['gx'=32,'gy'=16] {'gy'}, dimensions={0} | all-to-all | bytes 131072 | tf_op jit(solution)/shard_map/all_to_all | solution.py:436
  51.3 0.0 copy-start.2
  51.3 0.1 shard_map.160
  51.5 0.0 copy-start.6
  51.5 0.0 copy-start.9
  51.5 0.0 copy-start.10
  51.5 0.0 copy-start.11
  51.6 15.7 %all_to_all.48 = f32[32,1,1792]{2,1,0:T(1,128)S(1)} all-to-all(f32[32,1,1792]{2,1,0:T(1,128)S(1)} %bitcast.24), channel_id=1, replica_groups={{288,144,384,272,416,48,0,256,400,32,432,160,304,16,128,176,352,208,448..., dimensions={0} | all-to-all | bytes 458752 | tf_op jit(solution)/shard_map/all_to_all | solution.py:436
  67.3 0.0 copy-done
  67.3 0.0 copy-done.2
  67.3 0.0 copy-done.6
  67.3 0.0 copy-done.9
  67.3 0.0 copy-done.10
  67.3 0.0 copy-done.11
  67.3 0.8 %shard_map.161 = (f32[384,128]{1,0:T(8,128)S(1)}, f32[8,128]{1,0:T(8,128)S(1)}) custom-call(f32[448,128]{1,0:T(8,128)S(1)} %bitcast.25, bf16[2,32,192]{2,1,0:T(8,128)(2,1)S(1)} %copy-done.10, bf16[2,32,384]{2,1,0:T(8,128)(2,1)S(1)} %copy-done.6, bf16[768,256]{1,0:T(8,128)(2,1)S(1)} %copy-done.2, bf16[1536,256]{1,0:T(8,128)(2,1)S(1)} %copy-done, ...), custom_call_target="tpu_custom_call" | custom-call | flops 1000000 | bytes 1000000 | tf_op jit(solution)/shard_map/pallas_call | solution.py:475
  68.1 0.0 copy-start.3
  68.2 0.0 copy-start.4
  68.2 0.0 copy-start.5
  68.2 12.4 %all_to_all.49 = f32[16,1,3072]{2,1,0:T(1,128)S(1)} all-to-all(f32[16,1,3072]{2,1,0:T(1,128)S(1)} %bitcast.38), channel_id=1, replica_groups={{288,144,384,272,416,48,0,256,400,32,432,160,304,16,128,176},{352,208,4..., dimensions={0} | all-to-all | bytes 393216 | tf_op jit(solution)/shard_map/all_to_all | solution.py:436
  80.6 0.0 copy-done.3
  80.6 0.0 copy-done.4
  80.6 0.0 copy-done.5
  80.6 0.8 shard_map.162
Async XLA Ops:
  0.6 17.3 %copy-start.1 = (bf16[768,256]{1,0:T(8,128)(2,1)S(1)}, bf16[768,256]{1,0:T(8,128)(2,1)}, u32[]{:S(2)}) copy-start(bf16[768,256]{1,0:T(8,128)(2,1)} %constant.19.clone.along) | copy-start | bytes 1179652
  1.8 16.1 %copy-start.7 = (f32[2,32,128]{2,1,0:T(8,128)S(1)}, f32[2,32,128]{2,1,0:T(8,128)}, u32[]{:S(2)}) copy-start(f32[2,32,128]{2,1,0:T(8,128)} %constant.20.clone.turn) | copy-start | bytes 98308
  1.8 16.1 %copy-start.8 = (bf16[2,64,96]{2,1,0:T(8,128)(2,1)S(1)}, bf16[2,64,96]{2,1,0:T(8,128)(2,1)}, u32[]{:S(2)}) copy-start(bf16[2,64,96]{2,1,0:T(8,128)(2,1)} %constant.18.clone.across) | copy-start | bytes 73732
  32.9 34.3 %copy-start = (bf16[1536,256]{1,0:T(8,128)(2,1)S(1)}, bf16[1536,256]{1,0:T(8,128)(2,1)}, u32[]{:S(2)}) copy-start(bf16[1536,256]{1,0:T(8,128)(2,1)} %constant.24.clone.along_full) | copy-start | bytes 2359300
  51.3 15.9 %copy-start.2 = (bf16[768,256]{1,0:T(8,128)(2,1)S(1)}, bf16[768,256]{1,0:T(8,128)(2,1)}, u32[]{:S(2)}) copy-start(bf16[768,256]{1,0:T(8,128)(2,1)} %constant.23.clone.along) | copy-start | bytes 1179652
  51.5 15.8 %copy-start.6 = (bf16[2,32,384]{2,1,0:T(8,128)(2,1)S(1)}, bf16[2,32,384]{2,1,0:T(8,128)(2,1)}, u32[]{:S(2)}) copy-start(bf16[2,32,384]{2,1,0:T(8,128)(2,1)} %constant.22.clone.across_full) | copy-start | bytes 147460
  51.5 15.8 %copy-start.9 = (f32[2,32,128]{2,1,0:T(8,128)S(1)}, f32[2,32,128]{2,1,0:T(8,128)}, u32[]{:S(2)}) copy-start(f32[2,32,128]{2,1,0:T(8,128)} %constant.25.clone.turn) | copy-start | bytes 98308
  51.5 15.8 %copy-start.10 = (bf16[2,32,192]{2,1,0:T(8,128)(2,1)S(1)}, bf16[2,32,192]{2,1,0:T(8,128)(2,1)}, u32[]{:S(2)}) copy-start(bf16[2,32,192]{2,1,0:T(8,128)(2,1)} %constant.21.clone.across) | copy-start | bytes 73732
  51.5 15.8 %copy-start.11 = (f32[32,128]{1,0:T(8,128)S(1)}, f32[32,128]{1,0:T(8,128)}, u32[]{:S(2)}) copy-start(f32[32,128]{1,0:T(8,128)} %constant.26.clone.waves) | copy-start | bytes 49156
  68.1 12.5 %copy-start.3 = (f32[2,1,96,128]{3,2,1,0:T(8,128)S(1)}, f32[2,1,96,128]{3,2,1,0:T(8,128)}, u32[]{:S(2)}) copy-start(f32[2,1,96,128]{3,2,1,0:T(8,128)} %param.14) | copy-start | bytes 294916
  68.2 12.5 %copy-start.4 = (f32[2,1,96,128]{3,2,1,0:T(8,128)S(1)}, f32[2,1,96,128]{3,2,1,0:T(8,128)}, u32[]{:S(2)}) copy-start(f32[2,1,96,128]{3,2,1,0:T(8,128)} %param.15) | copy-start | bytes 294916
  68.2 12.5 %copy-start.5 = (f32[2,1,96,128]{3,2,1,0:T(8,128)S(1)}, f32[2,1,96,128]{3,2,1,0:T(8,128)}, u32[]{:S(2)}) copy-start(f32[2,1,96,128]{3,2,1,0:T(8,128)} %param.16) | copy-start | bytes 294916

commit v8 on v7

--- a/solution.py
+++ b/solution.py
@@ -364,10 +364,10 @@
         flow.append(jnp.concatenate([-kx * imag, kx * real], 1))
         plain.append(jnp.concatenate([real, imag], 1))
     plain.append(jnp.concatenate([slot(2 * per), slot(2 * per + 1)], 1))
+    flow = right_dot(jnp.concatenate(flow, 0), along[...], 2)
     plain = right_dot(jnp.concatenate(plain, 0), along_full[...], 3)
-    flow = right_dot(jnp.concatenate(flow, 0), along[...], 2)
+    flow = left_dot(across[group], turned(flow), 2)
     plain = left_dot(across_full[group], turned(plain), 3)
-    flow = left_dot(across[group], turned(flow), 2)
     for i, done in enumerate((flow, plain)):
         for part in range(2):
             for t in range(per):

time: 81.8 us -> 81.7 us (level)
  no operation moved by 1% of the time
where the time goes in v8:
time: 81.7 us; the launch traced here: 81.3 us
  blocking collectives  77 us (94%)
  Pallas kernels  3.54 us (4%)
    all_to_all x5, blocking collectives, exchange(): lax.all_to_all(array, axis, 0, 0, axis_index_groups=groups, tiled=True)  77 us

profile of v8, /device:TPU:4, one launch (start us, length us, event | category | flops | bytes accessed | tf_op | source)
XLA Modules:
  0.0 81.3 jit_solution(9061076885434773675)
XLA Ops:
  0.6 0.0 copy-start.1
  0.6 1.1 %shard_map.157 = (f32[416,128]{1,0:T(8,128)S(1)}, f32[96,128]{1,0:T(8,128)S(1)}, f32[96,128]{1,0:T(8,128)S(1)}) custom-call(f32[2,96,128]{2,1,0:T(8,128)} %bitcast.30, f32[2,96,128]{2,1,0:T(8,128)} %bitcast.32, f32[2,96,128]{2,1,0:T(8,128)} %bitcast.34, f32[1,96]{1,0:T(1,128)} %bitcast.40, f32[1,96]{1,0:T(1,128)} %bitcast.41), custom_call_target="tpu_custom_call" | custom-call | flops 1000000 | bytes 1000000 | tf_op jit(solution)/shard_map/pallas_call | solution.py:452
  1.8 0.0 copy-start.7
  1.8 0.0 copy-start.8
  1.8 16.1 %all_to_all.45 = f32[16,1,3328]{2,1,0:T(1,128)S(1)} all-to-all(f32[16,1,3328]{2,1,0:T(1,128)S(1)} %bitcast.37), channel_id=1, replica_groups={{288,144,48,160,304,384,0,32,176,256,432,272,416,128,16,400},{352,208,1..., dimensions={0} | all-to-all | bytes 425984 | tf_op jit(solution)/shard_map/all_to_all | solution.py:436
  17.9 0.0 copy-done.1
  17.9 0.0 copy-done.7
  17.9 0.0 copy-done.8
  17.9 0.5 shard_map.158
  18.4 14.5 %all_to_all.46 = f32[32,1,1664]{2,1,0:T(1,128)S(1)} all-to-all(f32[32,1,1664]{2,1,0:T(1,128)S(1)} %bitcast.27), channel_id=1, replica_groups={{288,144,48,160,304,384,0,32,176,256,432,272,416,128,16,400,352,208,112..., dimensions={0} | all-to-all | bytes 425984 | tf_op jit(solution)/shard_map/all_to_all | solution.py:436
  32.9 0.0 copy-start
  32.9 0.2 shard_map.159
  33.1 18.2 %all_to_all.47 = f32[16,1,1024]{2,1,0:T(1,128)S(1)} all-to-all(f32[16,1,1024]{2,1,0:T(1,128)S(1)} %bitcast.39), channel_id=1, replica_groups=mesh['gx'=32,'gy'=16] {'gy'}, dimensions={0} | all-to-all | bytes 131072 | tf_op jit(solution)/shard_map/all_to_all | solution.py:436
  51.3 0.0 copy-start.2
  51.3 0.1 shard_map.160
  51.5 0.0 copy-start.6
  51.5 0.0 copy-start.9
  51.5 0.0 copy-start.10
  51.5 0.0 copy-start.11
  51.6 15.7 %all_to_all.48 = f32[32,1,1792]{2,1,0:T(1,128)S(1)} all-to-all(f32[32,1,1792]{2,1,0:T(1,128)S(1)} %bitcast.24), channel_id=1, replica_groups={{288,144,384,272,416,48,0,256,400,32,432,160,304,16,128,176,352,208,448..., dimensions={0} | all-to-all | bytes 458752 | tf_op jit(solution)/shard_map/all_to_all | solution.py:436
  67.3 0.0 copy-done
  67.3 0.0 copy-done.2
  67.3 0.0 copy-done.6
  67.3 0.0 copy-done.9
  67.3 0.0 copy-done.10
  67.3 0.0 copy-done.11
  67.3 0.8 shard_map.161
  68.1 0.0 copy-start.3
  68.1 0.0 copy-start.4
  68.1 0.0 copy-start.5
  68.1 12.4 %all_to_all.49 = f32[16,1,3072]{2,1,0:T(1,128)S(1)} all-to-all(f32[16,1,3072]{2,1,0:T(1,128)S(1)} %bitcast.38), channel_id=1, replica_groups={{288,144,384,272,416,48,0,256,400,32,432,160,304,16,128,176},{352,208,4..., dimensions={0} | all-to-all | bytes 393216 | tf_op jit(solution)/shard_map/all_to_all | solution.py:436
  80.6 0.0 copy-done.3
  80.6 0.0 copy-done.4
  80.6 0.0 copy-done.5
  80.6 0.8 shard_map.162
Async XLA Ops:
  0.6 17.3 %copy-start.1 = (bf16[768,256]{1,0:T(8,128)(2,1)S(1)}, bf16[768,256]{1,0:T(8,128)(2,1)}, u32[]{:S(2)}) copy-start(bf16[768,256]{1,0:T(8,128)(2,1)} %constant.19.clone.along) | copy-start | bytes 1179652
  1.8 16.1 %copy-start.7 = (f32[2,32,128]{2,1,0:T(8,128)S(1)}, f32[2,32,128]{2,1,0:T(8,128)}, u32[]{:S(2)}) copy-start(f32[2,32,128]{2,1,0:T(8,128)} %constant.20.clone.turn) | copy-start | bytes 98308
  1.8 16.1 %copy-start.8 = (bf16[2,64,96]{2,1,0:T(8,128)(2,1)S(1)}, bf16[2,64,96]{2,1,0:T(8,128)(2,1)}, u32[]{:S(2)}) copy-start(bf16[2,64,96]{2,1,0:T(8,128)(2,1)} %constant.18.clone.across) | copy-start | bytes 73732
  32.9 34.3 %copy-start = (bf16[1536,256]{1,0:T(8,128)(2,1)S(1)}, bf16[1536,256]{1,0:T(8,128)(2,1)}, u32[]{:S(2)}) copy-start(bf16[1536,256]{1,0:T(8,128)(2,1)} %constant.24.clone.along_full) | copy-start | bytes 2359300
  51.3 15.9 %copy-start.2 = (bf16[768,256]{1,0:T(8,128)(2,1)S(1)}, bf16[768,256]{1,0:T(8,128)(2,1)}, u32[]{:S(2)}) copy-start(bf16[768,256]{1,0:T(8,128)(2,1)} %constant.23.clone.along) | copy-start | bytes 1179652
  51.5 15.8 %copy-start.6 = (bf16[2,32,384]{2,1,0:T(8,128)(2,1)S(1)}, bf16[2,32,384]{2,1,0:T(8,128)(2,1)}, u32[]{:S(2)}) copy-start(bf16[2,32,384]{2,1,0:T(8,128)(2,1)} %constant.22.clone.across_full) | copy-start | bytes 147460
  51.5 15.8 %copy-start.9 = (f32[2,32,128]{2,1,0:T(8,128)S(1)}, f32[2,32,128]{2,1,0:T(8,128)}, u32[]{:S(2)}) copy-start(f32[2,32,128]{2,1,0:T(8,128)} %constant.25.clone.turn) | copy-start | bytes 98308
  51.5 15.8 %copy-start.10 = (bf16[2,32,192]{2,1,0:T(8,128)(2,1)S(1)}, bf16[2,32,192]{2,1,0:T(8,128)(2,1)}, u32[]{:S(2)}) copy-start(bf16[2,32,192]{2,1,0:T(8,128)(2,1)} %constant.21.clone.across) | copy-start | bytes 73732
  51.5 15.8 %copy-start.11 = (f32[32,128]{1,0:T(8,128)S(1)}, f32[32,128]{1,0:T(8,128)}, u32[]{:S(2)}) copy-start(f32[32,128]{1,0:T(8,128)} %constant.26.clone.waves) | copy-start | bytes 49156
  68.1 12.5 %copy-start.3 = (f32[2,1,96,128]{3,2,1,0:T(8,128)S(1)}, f32[2,1,96,128]{3,2,1,0:T(8,128)}, u32[]{:S(2)}) copy-start(f32[2,1,96,128]{3,2,1,0:T(8,128)} %param.14) | copy-start | bytes 294916
  68.1 12.5 %copy-start.4 = (f32[2,1,96,128]{3,2,1,0:T(8,128)S(1)}, f32[2,1,96,128]{3,2,1,0:T(8,128)}, u32[]{:S(2)}) copy-start(f32[2,1,96,128]{3,2,1,0:T(8,128)} %param.15) | copy-start | bytes 294916
  68.1 12.5 %copy-start.5 = (f32[2,1,96,128]{3,2,1,0:T(8,128)S(1)}, f32[2,1,96,128]{3,2,1,0:T(8,128)}, u32[]{:S(2)}) copy-start(f32[2,1,96,128]{3,2,1,0:T(8,128)} %param.16) | copy-start | bytes 294916
